TPU v7x, 32 devices: a whole 2x2x4 slice. The times are simulated.
32 devices in a mesh: gx: 8 (over z, x), gy: 4 (over y, core).
Axes of the slice: x: 2, y: 2, z: 4, core: 2. Of those that a mesh axis runs over, the one named last changes fastest.
Arguments:
- volts_start: float32 [8, 128, 4096], P(None, 'gx', 'gy'), may hold values from 0.55 to 1, as said below
- seg_cond: float32 [8, 128, 4096], P(None, 'gx', 'gy'), may hold values from 0.5 to 2
- via_cond: float32 [7, 128, 4096], P(None, 'gx', 'gy'), may hold values from 1 to 4
- via_mask: int32 [7, 128, 4096], P(None, 'gx', 'gy'), may hold values 0 or 1
- pad_mask: int32 [128, 4096], P('gx', 'gy'), may hold values 0 or 1
- load_current: float32 [128, 4096], P('gx', 'gy'), may hold values from 0 to 2.7, as said below
- stress_start: float32 [8, 128, 4096], P(None, 'gx', 'gy'), may hold values from -6 to 6
- mobility: float32 [8, 128, 4096], P(None, 'gx', 'gy'), may hold values from 0.1 to 0.45
- blocked: int32 [8, 128, 4096], P(None, 'gx', 'gy'), may hold values 0 or 1
- layer_dirs: int32 [8], replicated, may hold values from 0 to 1, as said below
Outputs:
- volts_final: float32 [8, 128, 4096], P(None, 'gx', 'gy')
- stress_final: float32 [8, 128, 4096], P(None, 'gx', 'gy')
- resid_rms: float32 [], replicated
Inputs may be any that keep to these rules, and one draw needn't show every extreme that they name: `volts_start`: node voltages near the supply level, one sign. `load_current`: positive load currents. `layer_dirs`: exactly 4 layers run along x and the others along y.
All inputs are finite; a program needn't handle non-finite values. No bound on the sum of `via_mask` or of `pad_mask` or of `blocked` on one device may be relied on, other than what follows from the above.
Results may differ from a plain program's by a relative error of at most 0.00002.
Values sent between devices are 32-bit elements; how exact they have to be, the bound alone decides.
A program may use at most 64 MiB of HBM per device.

v0:
```python
import jax
import jax.numpy as jnp
from jax import lax
from jax.sharding import PartitionSpec as P

SWEEPS = 3
STEPS = 3


damping = 0.8
pad_conductance = 4.0
supply_volts = 1.0
wind_factor = 4.0


def from_behind(value, axis, steps):
    count = lax.axis_size(axis)
    initial, last = (max(0, -steps), min(count, count - steps))
    return lax.ppermute(value, axis, [(source, source + steps) for source in range(initial, last)])


def with_halo(cells, sides, width):
    for axis, dim in sides:
        count = lax.axis_size(axis)
        ends = count - 1
        head = lax.slice_in_dim(cells, 0, width, axis=dim)
        tail = lax.slice_in_dim(cells, cells.shape[dim] - width, cells.shape[dim], axis=dim)
        cells = jnp.concatenate(
            [
                lax.ppermute(tail, axis, [(i, (i + 1) % count) for i in range(ends)]),
                cells,
                lax.ppermute(head, axis, [((i + 1) % count, i) for i in range(ends)]),
            ],
            axis=dim,
        )
    return cells


def layer_pair(field):
    zero = jnp.zeros_like(field[:1])
    return (jnp.concatenate([zero, field[:-1]], 0), jnp.concatenate([field[1:], zero], 0))


def lateral_both(padded, cond_xl, cond_xr, cond_yl, cond_yr):
    total = cond_xl * padded[:, :-2, 1:-1] + cond_xr * padded[:, 2:, 1:-1]
    return total + cond_yl * padded[:, 1:-1, :-2] + cond_yr * padded[:, 1:-1, 2:]


def finish(lateral, volts, via_below, via_above, sources):
    below, above = layer_pair(volts)
    return lateral + via_below * below + via_above * above + sources


def body(
    volts_start,
    seg_cond,
    via_cond,
    via_mask,
    pad_mask,
    load_current,
    stress_start,
    mobility,
    blocked,
    layer_dirs,
):
    layers, rows_x, rows_y = seg_cond.shape
    total_x = rows_x * lax.axis_size("gx")
    total_y = rows_y * lax.axis_size("gy")
    index_x = lax.axis_index("gx") * rows_x + jnp.arange(rows_x, dtype=jnp.int32)
    index_y = lax.axis_index("gy") * rows_y + jnp.arange(rows_y, dtype=jnp.int32)
    inner_x = (index_x < total_x - 1).astype(jnp.float32)[None, :, None]
    inner_y = (index_y < total_y - 1).astype(jnp.float32)[None, None, :]
    along_y = layer_dirs.astype(jnp.float32)[:, None, None]
    along_x = 1.0 - along_y
    cond_xr = seg_cond * along_x * inner_x
    cond_yr = seg_cond * along_y * inner_y
    via_both = via_cond * via_mask.astype(jnp.float32)
    zero = jnp.zeros((1, rows_x, rows_y), jnp.float32)
    via_below = jnp.concatenate([zero, via_both], 0)
    via_above = jnp.concatenate([via_both, zero], 0)
    pads = pad_conductance * pad_mask.astype(jnp.float32)
    level = jnp.arange(layers)[:, None, None]
    top_cond = jnp.where(level == layers - 1, pads[None], jnp.float32(0.0))
    sources = top_cond * supply_volts - jnp.where(level == 0, load_current[None], jnp.float32(0.0))
    open_seg = 1.0 - blocked.astype(jnp.float32)
    mobile_x = mobility * open_seg * along_x * inner_x
    mobile_y = mobility * open_seg * along_y * inner_y
    edge_x = from_behind(jnp.stack([cond_xr[:, -1:, :], mobile_x[:, -1:, :]]), "gx", 1)
    edge_y = from_behind(jnp.stack([cond_yr[:, :, -1:], mobile_y[:, :, -1:]]), "gy", 1)
    cond_xl = jnp.concatenate([edge_x[0], cond_xr[:, :-1, :]], 1)
    mobile_xl = jnp.concatenate([edge_x[1], mobile_x[:, :-1, :]], 1)
    cond_yl = jnp.concatenate([edge_y[0], cond_yr[:, :, :-1]], 2)
    mobile_yl = jnp.concatenate([edge_y[1], mobile_y[:, :, :-1]], 2)
    diagonal = cond_xl + cond_xr + cond_yl + cond_yr + via_below + via_above + top_cond
    volts = volts_start
    for sweep in range(SWEEPS):
        padded = with_halo(volts, (("gx", 1), ("gy", 2)), 1)
        lateral = lateral_both(padded, cond_xl, cond_xr, cond_yl, cond_yr)
        volts = (1.0 - damping) * volts + damping * finish(
            lateral, volts, via_below, via_above, sources
        ) / diagonal
    padded = with_halo(volts, (("gx", 1), ("gy", 2)), 1)
    lateral = lateral_both(padded, cond_xl, cond_xr, cond_yl, cond_yr)
    current_x = cond_xr * (volts - padded[:, 2:, 1:-1])
    current_y = cond_yr * (volts - padded[:, 1:-1, 2:])
    current_xl = cond_xl * (padded[:, :-2, 1:-1] - volts)
    current_yl = cond_yl * (padded[:, 1:-1, :-2] - volts)
    resid = finish(lateral, volts, via_below, via_above, sources) - diagonal * volts
    squared = lax.psum(jnp.sum(resid * resid), ("gx", "gy"))
    resid_rms = jnp.sqrt(squared / (layers * total_x * total_y))
    wind_x = mobile_x * wind_factor * current_x
    wind_y = mobile_y * wind_factor * current_y
    wind_xl = mobile_xl * wind_factor * current_xl
    wind_yl = mobile_yl * wind_factor * current_yl
    drift = wind_x - wind_xl + wind_y - wind_yl
    stress = stress_start
    for step in range(STEPS):
        side = with_halo(stress, (("gx", 1), ("gy", 2)), 1)
        stress = (
            stress
            + mobile_x * (side[:, 2:, 1:-1] - stress)
            - mobile_xl * (stress - side[:, :-2, 1:-1])
            + mobile_y * (side[:, 1:-1, 2:] - stress)
            - mobile_yl * (stress - side[:, 1:-1, :-2])
            + drift
        )
    return (volts, stress, resid_rms)


def solution(mesh):
    in_specs = (
        P(None, "gx", "gy"),
        P(None, "gx", "gy"),
        P(None, "gx", "gy"),
        P(None, "gx", "gy"),
        P("gx", "gy"),
        P("gx", "gy"),
        P(None, "gx", "gy"),
        P(None, "gx", "gy"),
        P(None, "gx", "gy"),
        P(),
    )
    out_specs = (P(None, "gx", "gy"), P(None, "gx", "gy"), P())
    return jax.shard_map(body, mesh=mesh, in_specs=in_specs, out_specs=out_specs, check_vma=False)
```

profile of v0, /device:TPU:0, one launch (start us, length us, event | category | flops | bytes accessed | tf_op | source)
XLA Modules:
  0.0 178.0 jit_solution(16626624563301733297)
XLA Ops:
  1.3 1.8 %multiply_multiply_fusion.3 = (f32[8,16,1024]{2,1,0:T(8,128)S(1)}, f32[8,16,1024]{2,1,0:T(8,128)S(1)}, f32[8,16,1024]{2,1,0:T(8,128)S(1)}, f32[8,16,1024]{2,1,0:T(8,128)S(1)}) fusion(f32[8,16,1024]{2,1,0:T(8,128)} %param.11, f32[16]{0:T(128)S(1)} %compare_convert_fusion, f32[8]{0:T(128)S(1)} %broadcast_subtract_fusion, f32[1024]{0:T(1024)S(1)} %fusion.98, ...), kind=kLoop, calls=%fused_computation.174 | loop fusion | flops 1441792 | bytes 3674240 | tf_op jit(solution)/shard_map/mul | solution.py:75
  3.4 2.4 %collective-permute-start.3 = (f32[2,8,16,1]{2,1,3,0:T(8,128)S(1)}, f32[2,8,16,1]{2,1,3,0:T(8,128)S(1)}, u32[]{:S(2)}, u32[]{:S(2)}) collective-permute-start(f32[2,8,16,1]{2,1,3,0:T(8,128)S(1)} %pad_maximum_fusion.82), channel_id=1, source_target_pairs={{0,1},{1,2},{2,3},{4,5},{5,6},{6,7},{8,9},{9,10},{10,11},{12,13},{... | collective-permute-start | bytes 3080 | tf_op jit(solution)/shard_map/ppermute | solution.py:19
  5.9 4.2 %collective-permute-start = (f32[2,8,1,1024]{3,2,1,0:T(1,128)S(1)}, f32[2,8,1,1024]{3,2,1,0:T(1,128)S(1)}, u32[]{:S(2)}, u32[]{:S(2)}) collective-permute-start(f32[2,8,1,1024]{3,2,1,0:T(1,128)S(1)} %pad_maximum_fusion.81), channel_id=1, source_target_pairs={{0,4},{4,8},{8,12},{12,16},{16,20},{20,24},{24,28},{1,5},{5,9},{9,... | collective-permute-start | bytes 196616 | tf_op jit(solution)/shard_map/ppermute | solution.py:19
  10.2 3.5 %collective-permute-start.1 = (f32[8,1,1024]{2,1,0:T(1,128)S(1)}, f32[8,1,1024]{2,1,0:T(1,128)S(1)}, u32[]{:S(2)}, u32[]{:S(2)}) collective-permute-start(f32[8,1,1024]{2,1,0:T(1,128)S(1)} %get-tuple-element.49), channel_id=1, source_target_pairs={{0,4},{4,8},{8,12},{12,16},{16,20},{20,24},{24,28},{1,5},{5,9},{9,... | collective-permute-start | bytes 98312 | tf_op jit(solution)/shard_map/ppermute | solution.py:30
  13.7 1.4 collective-permute-start.2
  15.1 1.0 fusion.109
  16.4 3.3 %collective-permute-done.2 = f32[8,1,1024]{2,1,0:T(1,128)S(1)} collective-permute-done((f32[8,1,1024]{2,1,0:T(1,128)S(1)}, f32[8,1,1024]{2,1,0:T(1,128)S(1)}, u32[]{:S(2)}, u32[]{:S(2)}) %collective-permute-start.2) | collective-permute-done | bytes 32800 | tf_op jit(solution)/shard_map/ppermute | solution.py:32
  19.8 2.0 %collective-permute-start.4 = (f32[8,18,1]{2,1,0:T(8,128)S(1)}, f32[8,18,1]{2,1,0:T(8,128)S(1)}, u32[]{:S(2)}, u32[]{:S(2)}) collective-permute-start(f32[8,18,1]{2,1,0:T(8,128)S(1)} %get-tuple-element.25), channel_id=1, source_target_pairs={{0,1},{1,2},{2,3},{4,5},{5,6},{6,7},{8,9},{9,10},{10,11},{12,13},{... | collective-permute-start | bytes 1736 | tf_op jit(solution)/shard_map/ppermute | solution.py:30
  21.8 1.3 collective-permute-start.5
  23.2 3.0 %collective-permute-done.5 = f32[8,18,1]{2,1,0:T(8,128)S(1)} collective-permute-done((f32[8,18,1]{2,1,0:T(8,128)S(1)}, f32[8,18,1]{2,1,0:T(8,128)S(1)}, u32[]{:S(2)}, u32[]{:S(2)}) %collective-permute-start.5) | collective-permute-done | bytes 608 | tf_op jit(solution)/shard_map/ppermute | solution.py:32
  26.2 0.9 fusion.5
  27.1 4.3 %collective-permute-start.6 = (f32[8,1,1024]{2,1,0:T(1,128)S(1)}, f32[8,1,1024]{2,1,0:T(1,128)S(1)}, u32[]{:S(2)}, u32[]{:S(2)}) collective-permute-start(f32[8,1,1024]{2,1,0:T(1,128)S(1)} %get-tuple-element.43), channel_id=1, source_target_pairs={{0,4},{4,8},{8,12},{12,16},{16,20},{20,24},{24,28},{1,5},{5,9},{9,... | collective-permute-start | bytes 98312 | tf_op jit(solution)/shard_map/ppermute | solution.py:30
  31.4 1.3 collective-permute-start.7
  33.0 4.2 %collective-permute-done.7 = f32[8,1,1024]{2,1,0:T(1,128)S(1)} collective-permute-done((f32[8,1,1024]{2,1,0:T(1,128)S(1)}, f32[8,1,1024]{2,1,0:T(1,128)S(1)}, u32[]{:S(2)}, u32[]{:S(2)}) %collective-permute-start.7) | collective-permute-done | bytes 32800 | tf_op jit(solution)/shard_map/ppermute | solution.py:32
  37.4 3.7 %collective-permute-start.8 = (f32[8,18,1]{2,1,0:T(8,128)S(1)}, f32[8,18,1]{2,1,0:T(8,128)S(1)}, u32[]{:S(2)}, u32[]{:S(2)}) collective-permute-start(f32[8,18,1]{2,1,0:T(8,128)S(1)} %get-tuple-element.23), channel_id=1, source_target_pairs={{0,1},{1,2},{2,3},{4,5},{5,6},{6,7},{8,9},{9,10},{10,11},{12,13},{... | collective-permute-start | bytes 1736 | tf_op jit(solution)/shard_map/ppermute | solution.py:30
  41.1 1.3 collective-permute-start.9
  42.5 2.6 %collective-permute-done.9 = f32[8,18,1]{2,1,0:T(8,128)S(1)} collective-permute-done((f32[8,18,1]{2,1,0:T(8,128)S(1)}, f32[8,18,1]{2,1,0:T(8,128)S(1)}, u32[]{:S(2)}, u32[]{:S(2)}) %collective-permute-start.9) | collective-permute-done | bytes 608 | tf_op jit(solution)/shard_map/ppermute | solution.py:32
  45.1 0.9 fusion.11
  46.1 3.5 %collective-permute-start.10 = (f32[8,1,1024]{2,1,0:T(1,128)S(1)}, f32[8,1,1024]{2,1,0:T(1,128)S(1)}, u32[]{:S(2)}, u32[]{:S(2)}) collective-permute-start(f32[8,1,1024]{2,1,0:T(1,128)S(1)} %get-tuple-element.39), channel_id=1, source_target_pairs={{0,4},{4,8},{8,12},{12,16},{16,20},{20,24},{24,28},{1,5},{5,9},{9,... | collective-permute-start | bytes 98312 | tf_op jit(solution)/shard_map/ppermute | solution.py:30
  49.6 1.3 collective-permute-start.11
  50.9 1.3 collective-permute-start.14
  52.2 5.2 %collective-permute-start.15 = (f32[8,1,1024]{2,1,0:T(1,128)S(1)}, f32[8,1,1024]{2,1,0:T(1,128)S(1)}, u32[]{:S(2)}, u32[]{:S(2)}) collective-permute-start(f32[8,1,1024]{2,1,0:T(1,128)S(1)} %get-tuple-element.35), channel_id=1, source_target_pairs={{0,4},{4,8},{8,12},{12,16},{16,20},{20,24},{24,28},{1,5},{5,9},{9,... | collective-permute-start | bytes 98312 | tf_op jit(solution)/shard_map/ppermute | solution.py:30
  57.5 4.3 %collective-permute-start.12 = (f32[8,18,1]{2,1,0:T(8,128)S(1)}, f32[8,18,1]{2,1,0:T(8,128)S(1)}, u32[]{:S(2)}, u32[]{:S(2)}) collective-permute-start(f32[8,18,1]{2,1,0:T(8,128)S(1)} %get-tuple-element.21), channel_id=1, source_target_pairs={{0,1},{1,2},{2,3},{4,5},{5,6},{6,7},{8,9},{9,10},{10,11},{12,13},{... | collective-permute-start | bytes 1736 | tf_op jit(solution)/shard_map/ppermute | solution.py:30
  61.9 1.3 collective-permute-start.13
  63.3 2.0 %collective-permute-done.13 = f32[8,18,1]{2,1,0:T(8,128)S(1)} collective-permute-done((f32[8,18,1]{2,1,0:T(8,128)S(1)}, f32[8,18,1]{2,1,0:T(8,128)S(1)}, u32[]{:S(2)}, u32[]{:S(2)}) %collective-permute-start.13) | collective-permute-done | bytes 608 | tf_op jit(solution)/shard_map/ppermute | solution.py:32
  65.3 0.9 fusion.17
  66.3 1.3 collective-permute-start.18
  67.6 5.4 %collective-permute-start.19 = (f32[8,1,1024]{2,1,0:T(1,128)S(1)}, f32[8,1,1024]{2,1,0:T(1,128)S(1)}, u32[]{:S(2)}, u32[]{:S(2)}) collective-permute-start(f32[8,1,1024]{2,1,0:T(1,128)S(1)} %get-tuple-element.33), channel_id=1, source_target_pairs={{0,4},{4,8},{8,12},{12,16},{16,20},{20,24},{24,28},{1,5},{5,9},{9,... | collective-permute-start | bytes 98312 | tf_op jit(solution)/shard_map/ppermute | solution.py:30
  73.9 1.3 collective-permute-start.16
  75.1 6.1 %collective-permute-start.17 = (f32[8,18,1]{2,1,0:T(8,128)}, f32[8,18,1]{2,1,0:T(8,128)}, u32[]{:S(2)}, u32[]{:S(2)}) collective-permute-start(f32[8,18,1]{2,1,0:T(8,128)} %get-tuple-element.20), channel_id=1, source_target_pairs={{0,1},{1,2},{2,3},{4,5},{5,6},{6,7},{8,9},{9,10},{10,11},{12,13},{... | collective-permute-start | bytes 1736 | tf_op jit(solution)/shard_map/ppermute | solution.py:30
  82.0 1.3 collective-permute-start.20
  83.3 4.3 %collective-permute-start.21 = (f32[8,18,1]{2,1,0:T(8,128)}, f32[8,18,1]{2,1,0:T(8,128)}, u32[]{:S(2)}, u32[]{:S(2)}) collective-permute-start(f32[8,18,1]{2,1,0:T(8,128)} %get-tuple-element.18), channel_id=1, source_target_pairs={{0,1},{1,2},{2,3},{4,5},{5,6},{6,7},{8,9},{9,10},{10,11},{12,13},{... | collective-permute-start | bytes 1736 | tf_op jit(solution)/shard_map/ppermute | solution.py:30
  88.3 3.9 %fusion.67 = (f32[8,16,1024]{2,1,0:T(8,128)S(1)}, f32[8,16,1024]{2,1,0:T(8,128)S(1)}) fusion(f32[8,16,1024]{2,1,0:T(8,128)} %param.16, f32[8,18,1]{2,1,0:T(8,128)} %collective-permute-done.17, f32[8,1,1024]{2,1,0:T(1,128)} %copy-done.12, f32[8,1,1024]{2,1,0:T(1,128)} %copy-done.13, f32[8,16,1024]{2,1,0:T(8,128)S(1)} %get-tuple-element.56, ...), kind=kLoop, calls=%fused_computation.104 | loop fusion | flops 6815744 | bytes 6424832 | tf_op jit(solution)/shard_map/add | solution.py:120
  92.3 1.3 collective-permute-start.22
  93.6 5.2 %collective-permute-start.23 = (f32[8,1,1024]{2,1,0:T(1,128)S(1)}, f32[8,1,1024]{2,1,0:T(1,128)S(1)}, u32[]{:S(2)}, u32[]{:S(2)}) collective-permute-start(f32[8,1,1024]{2,1,0:T(1,128)S(1)} %get-tuple-element.31), channel_id=1, source_target_pairs={{0,4},{4,8},{8,12},{12,16},{16,20},{20,24},{24,28},{1,5},{5,9},{9,... | collective-permute-start | bytes 98312 | tf_op jit(solution)/shard_map/ppermute | solution.py:30
  98.7 1.6 collective-permute-done.23
  100.4 1.3 collective-permute-start.24
  101.7 4.1 %collective-permute-start.25 = (f32[8,18,1]{2,1,0:T(8,128)S(1)}, f32[8,18,1]{2,1,0:T(8,128)S(1)}, u32[]{:S(2)}, u32[]{:S(2)}) collective-permute-start(f32[8,18,1]{2,1,0:T(8,128)S(1)} %get-tuple-element.16), channel_id=1, source_target_pairs={{0,1},{1,2},{2,3},{4,5},{5,6},{6,7},{8,9},{9,10},{10,11},{12,13},{... | collective-permute-start | bytes 1736 | tf_op jit(solution)/shard_map/ppermute | solution.py:30
  105.8 0.9 collective-permute-done.25
  106.7 0.8 fusion.40
  107.6 1.3 collective-permute-start.26
  108.9 5.2 %collective-permute-start.27 = (f32[8,1,1024]{2,1,0:T(1,128)S(1)}, f32[8,1,1024]{2,1,0:T(1,128)S(1)}, u32[]{:S(2)}, u32[]{:S(2)}) collective-permute-start(f32[8,1,1024]{2,1,0:T(1,128)S(1)} %get-tuple-element.29), channel_id=1, source_target_pairs={{0,4},{4,8},{8,12},{12,16},{16,20},{20,24},{24,28},{1,5},{5,9},{9,... | collective-permute-start | bytes 98312 | tf_op jit(solution)/shard_map/ppermute | solution.py:30
  114.3 1.4 collective-permute-done.27
  116.5 1.3 collective-permute-start.28
  117.7 6.6 %collective-permute-start.29 = (f32[8,18,1]{2,1,0:T(8,128)}, f32[8,18,1]{2,1,0:T(8,128)}, u32[]{:S(2)}, u32[]{:S(2)}) collective-permute-start(f32[8,18,1]{2,1,0:T(8,128)} %get-tuple-element.14), channel_id=1, source_target_pairs={{0,1},{1,2},{2,3},{4,5},{5,6},{6,7},{8,9},{9,10},{10,11},{12,13},{... | collective-permute-start | bytes 1736 | tf_op jit(solution)/shard_map/ppermute | solution.py:30
  124.3 2.4 %fusion.23 = f32[]{:T(128)} fusion(f32[7,16,1024]{2,1,0:T(8,128)S(1)} %convert_multiply_fusion, f32[8,16,1024]{2,1,0:T(8,128)S(1)} %fusion.17, f32[8,1,1024]{2,1,0:T(1,128)S(1)} %copy-done.11, f32[8,16,1024]{2,1,0:T(8,128)S(1)} %get-tuple-element.47, f32[8,1,1024]{2,1,0:T(1,128)S(1)} %collective-permute-done.18, f32[7,16,1024]{2,1,0:T(8,128)S(1)} %get-tuple-element.28, ...), kind=kLoop, calls=%fused_computation.35 | loop fusion | flops 4587519 | bytes 4195476 | tf_op jit(solution)/shard_map/reduce_sum | solution.py:109
  126.7 45.8 %psum.7 = f32[]{:T(128)} all-reduce(f32[]{:T(128)} %fusion.23), channel_id=1, replica_groups=mesh['gx'=8,'gy'=4] {'gx','gy'}, use_global_device_ids=true, to_apply=%region_1.2 | all-reduce | flops 1 | bytes 8 | tf_op jit(solution)/shard_map/psum | solution.py:109
  173.2 3.6 %fusion.27 = f32[8,16,1024]{2,1,0:T(8,128)} fusion(f32[8,16,1024]{2,1,0:T(8,128)} %copy-done.3, f32[8,16,1024]{2,1,0:T(8,128)} %copy-done.2, f32[8,18,1]{2,1,0:T(8,128)} %collective-permute-done.29, f32[8,1,1024]{2,1,0:T(1,128)} %copy-done.14, f32[8,1,1024]{2,1,0:T(1,128)} %copy-done.15, f32[8,16,1024]{2,1,0:T(8,128)S(1)} %get-tuple-element.56, ...), kind=kLoop, calls=%fused_computation.40 | loop fusion | flops 3014656 | bytes 3736704 | tf_op jit(solution)/shard_map/add | solution.py:120
  (90 shorter events, 5.5 us)
Async XLA Ops:
  0.6 0.7 copy-start.17
  1.3 8.8 %copy-start.1 = (f32[8,16,1024]{2,1,0:T(8,128)S(1)}, f32[8,16,1024]{2,1,0:T(8,128)}, u32[]{:S(2)}) copy-start(f32[8,16,1024]{2,1,0:T(8,128)} %param.10) | copy-start | bytes 1572868
  3.4 12.9 %collective-permute-start.3 = (f32[2,8,16,1]{2,1,3,0:T(8,128)S(1)}, f32[2,8,16,1]{2,1,3,0:T(8,128)S(1)}, u32[]{:S(2)}, u32[]{:S(2)}) collective-permute-start(f32[2,8,16,1]{2,1,3,0:T(8,128)S(1)} %pad_maximum_fusion.82), channel_id=1, source_target_pairs={{0,1},{1,2},{2,3},{4,5},{5,6},{6,7},{8,9},{9,10},{10,11},{12,13},{... | collective-permute-start | bytes 3080 | tf_op jit(solution)/shard_map/ppermute | solution.py:19
  5.9 17.3 %collective-permute-start = (f32[2,8,1,1024]{3,2,1,0:T(1,128)S(1)}, f32[2,8,1,1024]{3,2,1,0:T(1,128)S(1)}, u32[]{:S(2)}, u32[]{:S(2)}) collective-permute-start(f32[2,8,1,1024]{3,2,1,0:T(1,128)S(1)} %pad_maximum_fusion.81), channel_id=1, source_target_pairs={{0,4},{4,8},{8,12},{12,16},{16,20},{20,24},{24,28},{1,5},{5,9},{9,... | collective-permute-start | bytes 196616 | tf_op jit(solution)/shard_map/ppermute | solution.py:19
  10.2 6.2 %collective-permute-start.1 = (f32[8,1,1024]{2,1,0:T(1,128)S(1)}, f32[8,1,1024]{2,1,0:T(1,128)S(1)}, u32[]{:S(2)}, u32[]{:S(2)}) collective-permute-start(f32[8,1,1024]{2,1,0:T(1,128)S(1)} %get-tuple-element.49), channel_id=1, source_target_pairs={{0,4},{4,8},{8,12},{12,16},{16,20},{20,24},{24,28},{1,5},{5,9},{9,... | collective-permute-start | bytes 98312 | tf_op jit(solution)/shard_map/ppermute | solution.py:30
  13.6 2.5 %copy-start.16 = (s32[16,1024]{1,0:T(8,128)S(1)}, s32[16,1024]{1,0:T(8,128)}, u32[]{:S(2)}) copy-start(s32[16,1024]{1,0:T(8,128)} %param.14) | copy-start | bytes 196612
  13.6 2.5 %copy-start.8 = (f32[7,16,1024]{2,1,0:T(8,128)S(1)}, f32[7,16,1024]{2,1,0:T(8,128)}, u32[]{:S(2)}) copy-start(f32[7,16,1024]{2,1,0:T(8,128)} %param.12) | copy-start | bytes 1376260
  13.6 2.5 %copy-start.9 = (s32[7,16,1024]{2,1,0:T(8,128)S(1)}, s32[7,16,1024]{2,1,0:T(8,128)}, u32[]{:S(2)}) copy-start(s32[7,16,1024]{2,1,0:T(8,128)} %param.13) | copy-start | bytes 1376260
  13.7 6.0 %collective-permute-start.2 = (f32[8,1,1024]{2,1,0:T(1,128)S(1)}, f32[8,1,1024]{2,1,0:T(1,128)S(1)}, u32[]{:S(2)}, u32[]{:S(2)}) collective-permute-start(f32[8,1,1024]{2,1,0:T(1,128)S(1)} %get-tuple-element.50), channel_id=1, source_target_pairs={{4,0},{8,4},{12,8},{16,12},{20,16},{24,20},{28,24},{5,1},{9,5},{13... | collective-permute-start | bytes 98312 | tf_op jit(solution)/shard_map/ppermute | solution.py:32
  16.2 9.9 %copy-start.7 = (f32[16,1024]{1,0:T(8,128)S(1)}, f32[16,1024]{1,0:T(8,128)}, u32[]{:S(2)}) copy-start(f32[16,1024]{1,0:T(8,128)} %param.15) | copy-start | bytes 196612
  16.4 9.8 %copy-start.5 = (f32[7,16,1024]{2,1,0:T(8,128)S(1)}, f32[7,16,1024]{2,1,0:T(8,128)}, u32[]{:S(2)}) copy-start(f32[7,16,1024]{2,1,0:T(8,128)} %get-tuple-element.45) | copy-start | bytes 1376260
  16.4 9.8 %copy-start.6 = (f32[7,16,1024]{2,1,0:T(8,128)S(1)}, f32[7,16,1024]{2,1,0:T(8,128)}, u32[]{:S(2)}) copy-start(f32[7,16,1024]{2,1,0:T(8,128)} %get-tuple-element.46) | copy-start | bytes 1376260
  19.8 3.4 %collective-permute-start.4 = (f32[8,18,1]{2,1,0:T(8,128)S(1)}, f32[8,18,1]{2,1,0:T(8,128)S(1)}, u32[]{:S(2)}, u32[]{:S(2)}) collective-permute-start(f32[8,18,1]{2,1,0:T(8,128)S(1)} %get-tuple-element.25), channel_id=1, source_target_pairs={{0,1},{1,2},{2,3},{4,5},{5,6},{6,7},{8,9},{9,10},{10,11},{12,13},{... | collective-permute-start | bytes 1736 | tf_op jit(solution)/shard_map/ppermute | solution.py:30
  21.8 4.3 %collective-permute-start.5 = (f32[8,18,1]{2,1,0:T(8,128)S(1)}, f32[8,18,1]{2,1,0:T(8,128)S(1)}, u32[]{:S(2)}, u32[]{:S(2)}) collective-permute-start(f32[8,18,1]{2,1,0:T(8,128)S(1)} %get-tuple-element.26), channel_id=1, source_target_pairs={{1,0},{2,1},{3,2},{5,4},{6,5},{7,6},{9,8},{10,9},{11,10},{13,12},{... | collective-permute-start | bytes 1736 | tf_op jit(solution)/shard_map/ppermute | solution.py:32
  27.1 5.9 %collective-permute-start.6 = (f32[8,1,1024]{2,1,0:T(1,128)S(1)}, f32[8,1,1024]{2,1,0:T(1,128)S(1)}, u32[]{:S(2)}, u32[]{:S(2)}) collective-permute-start(f32[8,1,1024]{2,1,0:T(1,128)S(1)} %get-tuple-element.43), channel_id=1, source_target_pairs={{0,4},{4,8},{8,12},{12,16},{16,20},{20,24},{24,28},{1,5},{5,9},{9,... | collective-permute-start | bytes 98312 | tf_op jit(solution)/shard_map/ppermute | solution.py:30
  31.4 5.8 %collective-permute-start.7 = (f32[8,1,1024]{2,1,0:T(1,128)S(1)}, f32[8,1,1024]{2,1,0:T(1,128)S(1)}, u32[]{:S(2)}, u32[]{:S(2)}) collective-permute-start(f32[8,1,1024]{2,1,0:T(1,128)S(1)} %get-tuple-element.44), channel_id=1, source_target_pairs={{4,0},{8,4},{12,8},{16,12},{20,16},{24,20},{28,24},{5,1},{9,5},{13... | collective-permute-start | bytes 98312 | tf_op jit(solution)/shard_map/ppermute | solution.py:32
  37.4 5.1 %collective-permute-start.8 = (f32[8,18,1]{2,1,0:T(8,128)S(1)}, f32[8,18,1]{2,1,0:T(8,128)S(1)}, u32[]{:S(2)}, u32[]{:S(2)}) collective-permute-start(f32[8,18,1]{2,1,0:T(8,128)S(1)} %get-tuple-element.23), channel_id=1, source_target_pairs={{0,1},{1,2},{2,3},{4,5},{5,6},{6,7},{8,9},{9,10},{10,11},{12,13},{... | collective-permute-start | bytes 1736 | tf_op jit(solution)/shard_map/ppermute | solution.py:30
  41.1 4.0 %collective-permute-start.9 = (f32[8,18,1]{2,1,0:T(8,128)S(1)}, f32[8,18,1]{2,1,0:T(8,128)S(1)}, u32[]{:S(2)}, u32[]{:S(2)}) collective-permute-start(f32[8,18,1]{2,1,0:T(8,128)S(1)} %get-tuple-element.24), channel_id=1, source_target_pairs={{1,0},{2,1},{3,2},{5,4},{6,5},{7,6},{9,8},{10,9},{11,10},{13,12},{... | collective-permute-start | bytes 1736 | tf_op jit(solution)/shard_map/ppermute | solution.py:32
  45.1 5.7 %copy-start.4 = (f32[8,16,1024]{2,1,0:T(8,128)S(1)}, f32[8,16,1024]{2,1,0:T(8,128)}, u32[]{:S(2)}) copy-start(f32[8,16,1024]{2,1,0:T(8,128)} %param.16) | copy-start | bytes 1572868
  46.1 11.3 %collective-permute-start.10 = (f32[8,1,1024]{2,1,0:T(1,128)S(1)}, f32[8,1,1024]{2,1,0:T(1,128)S(1)}, u32[]{:S(2)}, u32[]{:S(2)}) collective-permute-start(f32[8,1,1024]{2,1,0:T(1,128)S(1)} %get-tuple-element.39), channel_id=1, source_target_pairs={{0,4},{4,8},{8,12},{12,16},{16,20},{20,24},{24,28},{1,5},{5,9},{9,... | collective-permute-start | bytes 98312 | tf_op jit(solution)/shard_map/ppermute | solution.py:30
  49.6 7.9 %collective-permute-start.11 = (f32[8,1,1024]{2,1,0:T(1,128)S(1)}, f32[8,1,1024]{2,1,0:T(1,128)S(1)}, u32[]{:S(2)}, u32[]{:S(2)}) collective-permute-start(f32[8,1,1024]{2,1,0:T(1,128)S(1)} %get-tuple-element.40), channel_id=1, source_target_pairs={{4,0},{8,4},{12,8},{16,12},{20,16},{24,20},{28,24},{5,1},{9,5},{13... | collective-permute-start | bytes 98312 | tf_op jit(solution)/shard_map/ppermute | solution.py:32
  50.9 22.1 %collective-permute-start.14 = (f32[8,1,1024]{2,1,0:T(1,128)S(1)}, f32[8,1,1024]{2,1,0:T(1,128)S(1)}, u32[]{:S(2)}, u32[]{:S(2)}) collective-permute-start(f32[8,1,1024]{2,1,0:T(1,128)S(1)} %get-tuple-element.36), channel_id=1, source_target_pairs={{4,0},{8,4},{12,8},{16,12},{20,16},{24,20},{28,24},{5,1},{9,5},{13... | collective-permute-start | bytes 98312 | tf_op jit(solution)/shard_map/ppermute | solution.py:32
  52.2 20.9 %collective-permute-start.15 = (f32[8,1,1024]{2,1,0:T(1,128)S(1)}, f32[8,1,1024]{2,1,0:T(1,128)S(1)}, u32[]{:S(2)}, u32[]{:S(2)}) collective-permute-start(f32[8,1,1024]{2,1,0:T(1,128)S(1)} %get-tuple-element.35), channel_id=1, source_target_pairs={{0,4},{4,8},{8,12},{12,16},{16,20},{20,24},{24,28},{1,5},{5,9},{9,... | collective-permute-start | bytes 98312 | tf_op jit(solution)/shard_map/ppermute | solution.py:30
  57.5 5.7 %collective-permute-start.12 = (f32[8,18,1]{2,1,0:T(8,128)S(1)}, f32[8,18,1]{2,1,0:T(8,128)S(1)}, u32[]{:S(2)}, u32[]{:S(2)}) collective-permute-start(f32[8,18,1]{2,1,0:T(8,128)S(1)} %get-tuple-element.21), channel_id=1, source_target_pairs={{0,1},{1,2},{2,3},{4,5},{5,6},{6,7},{8,9},{9,10},{10,11},{12,13},{... | collective-permute-start | bytes 1736 | tf_op jit(solution)/shard_map/ppermute | solution.py:30
  61.9 3.5 %collective-permute-start.13 = (f32[8,18,1]{2,1,0:T(8,128)S(1)}, f32[8,18,1]{2,1,0:T(8,128)S(1)}, u32[]{:S(2)}, u32[]{:S(2)}) collective-permute-start(f32[8,18,1]{2,1,0:T(8,128)S(1)} %get-tuple-element.22), channel_id=1, source_target_pairs={{1,0},{2,1},{3,2},{5,4},{6,5},{7,6},{9,8},{10,9},{11,10},{13,12},{... | collective-permute-start | bytes 1736 | tf_op jit(solution)/shard_map/ppermute | solution.py:32
  66.2 58.1 %copy-start = (f32[8,16,1024]{2,1,0:T(8,128)}, f32[8,16,1024]{2,1,0:T(8,128)S(1)}, u32[]{:S(2)}) copy-start(f32[8,16,1024]{2,1,0:T(8,128)S(1)} %fusion.17) | copy-start | bytes 1572868
  66.3 15.0 %collective-permute-start.18 = (f32[8,1,1024]{2,1,0:T(1,128)S(1)}, f32[8,1,1024]{2,1,0:T(1,128)S(1)}, u32[]{:S(2)}, u32[]{:S(2)}) collective-permute-start(f32[8,1,1024]{2,1,0:T(1,128)S(1)} %get-tuple-element.34), channel_id=1, source_target_pairs={{4,0},{8,4},{12,8},{16,12},{20,16},{24,20},{28,24},{5,1},{9,5},{13... | collective-permute-start | bytes 98312 | tf_op jit(solution)/shard_map/ppermute | solution.py:32
  67.6 13.7 %collective-permute-start.19 = (f32[8,1,1024]{2,1,0:T(1,128)S(1)}, f32[8,1,1024]{2,1,0:T(1,128)S(1)}, u32[]{:S(2)}, u32[]{:S(2)}) collective-permute-start(f32[8,1,1024]{2,1,0:T(1,128)S(1)} %get-tuple-element.33), channel_id=1, source_target_pairs={{0,4},{4,8},{8,12},{12,16},{16,20},{20,24},{24,28},{1,5},{5,9},{9,... | collective-permute-start | bytes 98312 | tf_op jit(solution)/shard_map/ppermute | solution.py:30
  73.1 0.8 copy-start.12
  73.1 0.8 copy-start.13
  73.9 13.9 %collective-permute-start.16 = (f32[8,18,1]{2,1,0:T(8,128)}, f32[8,18,1]{2,1,0:T(8,128)}, u32[]{:S(2)}, u32[]{:S(2)}) collective-permute-start(f32[8,18,1]{2,1,0:T(8,128)} %get-tuple-element.19), channel_id=1, source_target_pairs={{1,0},{2,1},{3,2},{5,4},{6,5},{7,6},{9,8},{10,9},{11,10},{13,12},{... | collective-permute-start | bytes 1736 | tf_op jit(solution)/shard_map/ppermute | solution.py:32
  75.1 12.6 %collective-permute-start.17 = (f32[8,18,1]{2,1,0:T(8,128)}, f32[8,18,1]{2,1,0:T(8,128)}, u32[]{:S(2)}, u32[]{:S(2)}) collective-permute-start(f32[8,18,1]{2,1,0:T(8,128)} %get-tuple-element.20), channel_id=1, source_target_pairs={{0,1},{1,2},{2,3},{4,5},{5,6},{6,7},{8,9},{9,10},{10,11},{12,13},{... | collective-permute-start | bytes 1736 | tf_op jit(solution)/shard_map/ppermute | solution.py:30
  81.3 0.8 copy-start.10
  82.0 5.7 %collective-permute-start.20 = (f32[8,18,1]{2,1,0:T(8,128)}, f32[8,18,1]{2,1,0:T(8,128)S(1)}, u32[]{:S(2)}, u32[]{:S(2)}) collective-permute-start(f32[8,18,1]{2,1,0:T(8,128)} %get-tuple-element.17), channel_id=1, source_target_pairs={{1,0},{2,1},{3,2},{5,4},{6,5},{7,6},{9,8},{10,9},{11,10},{13,12},{... | collective-permute-start | bytes 1736 | tf_op jit(solution)/shard_map/ppermute | solution.py:32
  83.3 4.9 %collective-permute-start.21 = (f32[8,18,1]{2,1,0:T(8,128)}, f32[8,18,1]{2,1,0:T(8,128)}, u32[]{:S(2)}, u32[]{:S(2)}) collective-permute-start(f32[8,18,1]{2,1,0:T(8,128)} %get-tuple-element.18), channel_id=1, source_target_pairs={{0,1},{1,2},{2,3},{4,5},{5,6},{6,7},{8,9},{9,10},{10,11},{12,13},{... | collective-permute-start | bytes 1736 | tf_op jit(solution)/shard_map/ppermute | solution.py:30
  92.2 15.4 %copy-start.3 = (f32[8,16,1024]{2,1,0:T(8,128)}, f32[8,16,1024]{2,1,0:T(8,128)S(1)}, u32[]{:S(2)}) copy-start(f32[8,16,1024]{2,1,0:T(8,128)S(1)} %get-tuple-element.10) | copy-start | bytes 1572868
  92.3 6.5 %collective-permute-start.22 = (f32[8,1,1024]{2,1,0:T(1,128)S(1)}, f32[8,1,1024]{2,1,0:T(1,128)S(1)}, u32[]{:S(2)}, u32[]{:S(2)}) collective-permute-start(f32[8,1,1024]{2,1,0:T(1,128)S(1)} %get-tuple-element.32), channel_id=1, source_target_pairs={{4,0},{8,4},{12,8},{16,12},{20,16},{24,20},{28,24},{5,1},{9,5},{13... | collective-permute-start | bytes 98312 | tf_op jit(solution)/shard_map/ppermute | solution.py:32
  93.6 6.8 %collective-permute-start.23 = (f32[8,1,1024]{2,1,0:T(1,128)S(1)}, f32[8,1,1024]{2,1,0:T(1,128)S(1)}, u32[]{:S(2)}, u32[]{:S(2)}) collective-permute-start(f32[8,1,1024]{2,1,0:T(1,128)S(1)} %get-tuple-element.31), channel_id=1, source_target_pairs={{0,4},{4,8},{8,12},{12,16},{16,20},{20,24},{24,28},{1,5},{5,9},{9,... | collective-permute-start | bytes 98312 | tf_op jit(solution)/shard_map/ppermute | solution.py:30
  100.4 5.4 %collective-permute-start.24 = (f32[8,18,1]{2,1,0:T(8,128)S(1)}, f32[8,18,1]{2,1,0:T(8,128)S(1)}, u32[]{:S(2)}, u32[]{:S(2)}) collective-permute-start(f32[8,18,1]{2,1,0:T(8,128)S(1)} %get-tuple-element.15), channel_id=1, source_target_pairs={{1,0},{2,1},{3,2},{5,4},{6,5},{7,6},{9,8},{10,9},{11,10},{13,12},{... | collective-permute-start | bytes 1736 | tf_op jit(solution)/shard_map/ppermute | solution.py:32
  101.7 5.0 %collective-permute-start.25 = (f32[8,18,1]{2,1,0:T(8,128)S(1)}, f32[8,18,1]{2,1,0:T(8,128)S(1)}, u32[]{:S(2)}, u32[]{:S(2)}) collective-permute-start(f32[8,18,1]{2,1,0:T(8,128)S(1)} %get-tuple-element.16), channel_id=1, source_target_pairs={{0,1},{1,2},{2,3},{4,5},{5,6},{6,7},{8,9},{9,10},{10,11},{12,13},{... | collective-permute-start | bytes 1736 | tf_op jit(solution)/shard_map/ppermute | solution.py:30
  107.6 8.1 %copy-start.2 = (f32[8,16,1024]{2,1,0:T(8,128)}, f32[8,16,1024]{2,1,0:T(8,128)S(1)}, u32[]{:S(2)}) copy-start(f32[8,16,1024]{2,1,0:T(8,128)S(1)} %fusion.40) | copy-start | bytes 1572868
  107.6 6.6 %collective-permute-start.26 = (f32[8,1,1024]{2,1,0:T(1,128)S(1)}, f32[8,1,1024]{2,1,0:T(1,128)S(1)}, u32[]{:S(2)}, u32[]{:S(2)}) collective-permute-start(f32[8,1,1024]{2,1,0:T(1,128)S(1)} %get-tuple-element.30), channel_id=1, source_target_pairs={{4,0},{8,4},{12,8},{16,12},{20,16},{24,20},{28,24},{5,1},{9,5},{13... | collective-permute-start | bytes 98312 | tf_op jit(solution)/shard_map/ppermute | solution.py:32
  108.9 6.8 %collective-permute-start.27 = (f32[8,1,1024]{2,1,0:T(1,128)S(1)}, f32[8,1,1024]{2,1,0:T(1,128)S(1)}, u32[]{:S(2)}, u32[]{:S(2)}) collective-permute-start(f32[8,1,1024]{2,1,0:T(1,128)S(1)} %get-tuple-element.29), channel_id=1, source_target_pairs={{0,4},{4,8},{8,12},{12,16},{16,20},{20,24},{24,28},{1,5},{5,9},{9,... | collective-permute-start | bytes 98312 | tf_op jit(solution)/shard_map/ppermute | solution.py:30
  114.2 10.1 %copy-start.11 = (f32[8,1,1024]{2,1,0:T(1,128)S(1)}, f32[8,1,1024]{2,1,0:T(1,128)}, u32[]{:S(2)}) copy-start(f32[8,1,1024]{2,1,0:T(1,128)} %copy-done.10) | copy-start | bytes 98308
  114.2 2.2 %copy-start.14 = (f32[8,1,1024]{2,1,0:T(1,128)}, f32[8,1,1024]{2,1,0:T(1,128)S(1)}, u32[]{:S(2)}) copy-start(f32[8,1,1024]{2,1,0:T(1,128)S(1)} %collective-permute-done.26) | copy-start | bytes 98308
  115.7 0.8 copy-start.15
  116.5 56.8 %collective-permute-start.28 = (f32[8,18,1]{2,1,0:T(8,128)}, f32[8,18,1]{2,1,0:T(8,128)}, u32[]{:S(2)}, u32[]{:S(2)}) collective-permute-start(f32[8,18,1]{2,1,0:T(8,128)} %get-tuple-element.13), channel_id=1, source_target_pairs={{1,0},{2,1},{3,2},{5,4},{6,5},{7,6},{9,8},{10,9},{11,10},{13,12},{... | collective-permute-start | bytes 1736 | tf_op jit(solution)/shard_map/ppermute | solution.py:32
  117.7 55.5 %collective-permute-start.29 = (f32[8,18,1]{2,1,0:T(8,128)}, f32[8,18,1]{2,1,0:T(8,128)}, u32[]{:S(2)}, u32[]{:S(2)}) collective-permute-start(f32[8,18,1]{2,1,0:T(8,128)} %get-tuple-element.14), channel_id=1, source_target_pairs={{0,1},{1,2},{2,3},{4,5},{5,6},{6,7},{8,9},{9,10},{10,11},{12,13},{... | collective-permute-start | bytes 1736 | tf_op jit(solution)/shard_map/ppermute | solution.py:30
where the time goes:
time: 179 us; the launch traced here: 178 us
  starting transfers between devices  88.1 us (49%)
  blocking collectives  45.8 us (26%)
  waiting for transfers between devices  19.9 us (11%)
  other arithmetic  18.1 us (10%)
  between operations  3.18 us (2%)
  local copies, waits for them, and re-layouts  2.91 us (2%)
    ppermute x14, starting transfers between devices, with_halo(): lax.ppermute(tail, axis, [(i, (i + 1) % count) for i in range(ends)])  63.3 us
    psum x1, blocking collectives, body(): squared = lax.psum(jnp.sum(resid * resid), ('gx', 'gy'))  45.8 us
    ppermute x14, starting transfers between devices, with_halo(): lax.ppermute(head, axis, [((i + 1) % count, i) for i in range(ends)])  18.2 us
    ppermute x14, waiting for transfers between devices, with_halo(): lax.ppermute(head, axis, [((i + 1) % count, i) for i in range(ends)])  15.2 us
    add x3, other arithmetic, body(): stress + mobile_x * (side[:, 2:, 1:-1] - stress)  8.37 us
    ppermute x2, starting transfers between devices, from_behind(): lax.ppermute(value, axis, [(source, source + steps) for source in range(i...  6.58 us
    ppermute x14, waiting for transfers between devices, with_halo(): lax.ppermute(tail, axis, [(i, (i + 1) % count) for i in range(ends)])  4.71 us
  transfers between devices with their start and end apart: 30, of which 10 were waited for; matrix products, arithmetic and copies ran while one was open for 4% of the time, Pallas kernels for 0%

commit v1 on v0

v1 whole, which is shorter than its diff:
```python
import functools
import jax
import jax.numpy as jnp
from jax import lax
from jax.experimental import pallas as pl
from jax.experimental.pallas import tpu as pltpu
from jax.sharding import PartitionSpec as P

damping = 0.8
pad_conductance = 4.0
supply_volts = 1.0
wind_factor = 4.0

MESH = pl.DeviceIdType.MESH
VOLTS, STRESS, PARTIAL, VOLTS2, STRESS1 = range(5)
ROUNDS = 5


def kernel(
    n_x, n_y, layers, rows_x, rows_y,
    dirs, volts_hbm, seg_hbm, via_hbm, vmask_hbm, pad_hbm, load_hbm, stress_hbm, mob_hbm, blk_hbm,
    volts_out, stress_out, rms_out,
    volts_in, seg_in, via_in, vmask_in, pad_in, load_in, stress_in, mob_in, blk_in,
    cond_r, cond_l, via_b, via_a, source, diag, weight, partial,
    mob_r, mob_l, wind_r, wind_l, volts_a, volts_b, stress_a, volts_fin, stress_fin,
    send_x, recv_x, send_y, recv_y, sum_x, sum_y,
    in_sem, out_sem, send_sem, recv_sem, sx_send, sx_recv, sy_send, sy_recv,
):
    half = layers // 2
    gx = lax.axis_index("gx")
    gy = lax.axis_index("gy")

    moves = [
        pltpu.make_async_copy(src, dst, in_sem.at[i])
        for i, (src, dst) in enumerate(
            [
                (volts_hbm, volts_in), (seg_hbm, seg_in), (via_hbm, via_in), (vmask_hbm, vmask_in), (pad_hbm, pad_in),
                (load_hbm, load_in), (stress_hbm, stress_in), (mob_hbm, mob_in), (blk_hbm, blk_in),
            ]
        )
    ]
    for move in moves:
        move.start()

    barrier = pltpu.get_barrier_semaphore()
    for o in range(1, n_x):
        pl.semaphore_signal(barrier, inc=1, device_id=(lax.rem(gx + o, n_x), gy), device_id_type=MESH)
    for o in range(1, n_y):
        pl.semaphore_signal(barrier, inc=1, device_id=(gx, lax.rem(gy + o, n_y)), device_id_type=MESH)

    to_has = [gx < n_x - 1, gx > 0, gy < n_y - 1, gy > 0]
    from_has = [gx > 0, gx < n_x - 1, gy > 0, gy < n_y - 1]
    target = [
        (jnp.minimum(gx + 1, n_x - 1), gy), (jnp.maximum(gx - 1, 0), gy),
        (gx, jnp.minimum(gy + 1, n_y - 1)), (gx, jnp.maximum(gy - 1, 0)),
    ]

    def edge_copy(r, d):
        if d < 2:
            count = 1 if (d == 1 and r in (VOLTS, STRESS)) else 2
            src, dst = send_x.at[r, d, 0:count], recv_x.at[r, d, 0:count]
        else:
            src, dst = send_y.at[r, d - 2], recv_y.at[r, d - 2]
        return pltpu.make_async_remote_copy(
            src_ref=src, dst_ref=dst, send_sem=send_sem.at[r, d], recv_sem=recv_sem.at[r, d],
            device_id=target[d], device_id_type=MESH,
        )

    def start(r):
        for d in range(4):
            @pl.when(to_has[d])
            def _():
                edge_copy(r, d).start()

    def arrive(r):
        for d in range(4):
            @pl.when(from_has[d])
            def _():
                edge_copy(r, d).wait_recv()

    for d in range(2):
        @pl.when(jnp.logical_not(from_has[d]))
        def _():
            for r in range(ROUNDS):
                recv_x[r, d] = jnp.full(recv_x.shape[2:], 1.0 if r == PARTIAL else 0.0, jnp.float32)

        @pl.when(jnp.logical_not(from_has[d + 2]))
        def _():
            for r in range(ROUNDS):
                recv_y[r, d] = jnp.full(recv_y.shape[2:], 1.0 if r == PARTIAL else 0.0, jnp.float32)

    is_y = [dirs[l] for l in range(layers)]
    pos = []
    seen_x, seen_y = jnp.int32(0), jnp.int32(half)
    for l in range(layers):
        pos.append(jnp.where(is_y[l] == 1, seen_y, seen_x))
        seen_y = seen_y + is_y[l]
        seen_x = seen_x + 1 - is_y[l]
    layer = []
    for k in range(layers):
        at = jnp.int32(0)
        for l in range(1, layers):
            at = at + jnp.where(pos[l] == k, l, 0)
        layer.append(at)

    def slot_of(want):
        at = jnp.int32(0)
        for k in range(1, layers):
            at = at + jnp.where(layer[k] == want, k, 0)
        return at

    below = [jnp.maximum(layer[k] - 1, 0) for k in range(layers)]
    above = [jnp.minimum(layer[k] + 1, layers - 1) for k in range(layers)]
    slot_below = [slot_of(below[k]) for k in range(layers)]
    slot_above = [slot_of(above[k]) for k in range(layers)]

    shape = (rows_x, rows_y)
    index = [lax.broadcasted_iota(jnp.int32, shape, 0), lax.broadcasted_iota(jnp.int32, shape, 1)]
    length = [rows_x, rows_y]
    is_first = [index[0] == 0, index[1] == 0]
    is_last = [index[0] == rows_x - 1, index[1] == rows_y - 1]
    outer = [
        jnp.logical_and(is_last[0], gx == n_x - 1),
        jnp.logical_and(is_last[1], gy == n_y - 1),
    ]
    lane = lax.broadcasted_iota(jnp.int32, (rows_x, 128), 1)

    def axis_of(k):
        return 0 if k < half else 1

    def before(a, h, axis):
        return jnp.where(is_first[axis], h, pltpu.roll(a, 1, axis))

    def after(a, h, axis):
        return jnp.where(is_last[axis], h, pltpu.roll(a, length[axis] - 1, axis))

    def first(a, axis):
        return a[0:1, :] if axis == 0 else a[:, 0:1]

    def last(a, axis):
        return a[rows_x - 1:rows_x, :] if axis == 0 else a[:, rows_y - 1:rows_y]

    def put(r, k, to_next, to_prev):
        for d, values in ((0, to_next), (1, to_prev)):
            if k < half:
                for i, value in enumerate(values):
                    send_x[r, d, i, k:k + 1, :] = value
            else:
                packed = jnp.broadcast_to(values[0], (rows_x, 128))
                if len(values) > 1:
                    packed = jnp.where(lane == 0, packed, values[1])
                send_y[r, d, k - half] = packed

    def halo(r, k, d, i):
        if k < half:
            return recv_x[r, d, i, k:k + 1, :]
        return recv_y[r, d, k - half, :, i:i + 1]

    moves[0].wait()
    moves[1].wait()
    for k in range(layers):
        axis = axis_of(k)
        cr = jnp.where(outer[axis], 0.0, seg_in[layer[k]])
        cond_r[k] = cr
        cond_l[k] = before(cr, 0.0, axis)
        v = volts_in[layer[k]]
        put(VOLTS, k, [last(v, axis), last(cr, axis)], [first(v, axis)])
    pl.semaphore_wait(barrier, n_x + n_y - 2)
    start(VOLTS)

    for move in moves[2:6]:
        move.wait()
    pads = pad_conductance * pad_in[...].astype(jnp.float32)
    load = load_in[...]
    for k in range(layers):
        axis = axis_of(k)
        l = layer[k]
        up = jnp.minimum(l, layers - 2)
        va = via_in[up] * vmask_in[up].astype(jnp.float32) * jnp.where(l < layers - 1, 1.0, 0.0)
        vb = via_in[below[k]] * vmask_in[below[k]].astype(jnp.float32) * jnp.where(l > 0, 1.0, 0.0)
        top = pads * jnp.where(l == layers - 1, 1.0, 0.0)
        src = top * supply_volts - load * jnp.where(l == 0, 1.0, 0.0)
        via_a[k] = va
        via_b[k] = vb
        source[k] = src
        v = volts_in[l]
        cl, cr = cond_l[k], cond_r[k]
        dg = cl + cr + va + vb + top
        num = cl * before(v, 0.0, axis) + cr * after(v, 0.0, axis) + vb * volts_in[below[k]] + va * volts_in[above[k]] + src
        diag[k] = dg
        partial[k] = num
        put(PARTIAL, k, [last(num, axis), last(dg, axis)], [first(num, axis), first(dg, axis)])
    start(PARTIAL)

    for move in moves[6:]:
        move.wait()
    for k in range(layers):
        axis = axis_of(k)
        l = layer[k]
        mr = jnp.where(outer[axis], 0.0, mob_in[l] * (1.0 - blk_in[l].astype(jnp.float32)))
        mob_r[k] = mr
        s = stress_in[l]
        put(STRESS, k, [last(s, axis), last(mr, axis)], [first(s, axis)])
    start(STRESS)

    def edge_next(k, v_prev, n_prev, v_next, n_next, v):
        axis = axis_of(k)
        c_in, c_out = halo(VOLTS, k, 0, 1), last(cond_r[k], axis)
        h_prev = (1.0 - damping) * v_prev + damping * (n_prev + c_in * first(v, axis)) / halo(PARTIAL, k, 0, 1)
        h_next = (1.0 - damping) * v_next + damping * (n_next + c_out * last(v, axis)) / (halo(PARTIAL, k, 1, 1) + c_out)
        return h_prev, h_next

    arrive(VOLTS)
    for k in range(layers):
        axis = axis_of(k)
        c_in = halo(VOLTS, k, 0, 1)
        cl = jnp.where(is_first[axis], c_in, cond_l[k])
        cond_l[k] = cl
        dg = diag[k] + jnp.where(is_first[axis], c_in, 0.0)
        diag[k] = dg
        w = damping / dg
        weight[k] = w
        num = partial[k] + jnp.where(is_first[axis], c_in * halo(VOLTS, k, 0, 0), 0.0)
        num = num + jnp.where(is_last[axis], cond_r[k] * halo(VOLTS, k, 1, 0), 0.0)
        volts_a[k] = (1.0 - damping) * volts_in[layer[k]] + w * num

    def inflow(v_ref, k, v, h_prev, h_next):
        axis = axis_of(k)
        lateral = cond_l[k] * before(v, h_prev, axis) + cond_r[k] * after(v, h_next, axis)
        return lateral + via_b[k] * v_ref[slot_below[k]] + via_a[k] * v_ref[slot_above[k]] + source[k]

    arrive(PARTIAL)
    for k in range(layers):
        v = volts_a[k]
        h_prev, h_next = edge_next(
            k, halo(VOLTS, k, 0, 0), halo(PARTIAL, k, 0, 0), halo(VOLTS, k, 1, 0), halo(PARTIAL, k, 1, 0),
            volts_in[layer[k]],
        )
        volts_b[k] = (1.0 - damping) * v + weight[k] * inflow(volts_a, k, v, h_prev, h_next)
    for k in range(layers):
        axis = axis_of(k)
        v = volts_b[k]
        num = inflow(volts_b, k, v, 0.0, 0.0)
        partial[k] = num
        put(VOLTS2, k, [last(v, axis), last(num, axis)], [first(v, axis), first(num, axis)])
    start(VOLTS2)

    arrive(STRESS)
    for k in range(layers):
        axis = axis_of(k)
        mr = mob_r[k]
        ml = before(mr, halo(STRESS, k, 0, 1), axis)
        mob_l[k] = ml
        wind_r[k] = wind_factor * mr * cond_r[k]
        wind_l[k] = wind_factor * ml * cond_l[k]

    arrive(VOLTS2)
    for k in range(layers):
        axis = axis_of(k)
        num = partial[k] + jnp.where(is_first[axis], cond_l[k] * halo(VOLTS2, k, 0, 0), 0.0)
        num = num + jnp.where(is_last[axis], cond_r[k] * halo(VOLTS2, k, 1, 0), 0.0)
        volts_a[k] = (1.0 - damping) * volts_b[k] + weight[k] * num

    total = jnp.zeros(shape, jnp.float32)
    for k in range(layers):
        axis = axis_of(k)
        v = volts_a[k]
        h_prev, h_next = edge_next(
            k, halo(VOLTS2, k, 0, 0), halo(VOLTS2, k, 0, 1), halo(VOLTS2, k, 1, 0), halo(VOLTS2, k, 1, 1), volts_b[k]
        )
        v_prev, v_next = before(v, h_prev, axis), after(v, h_next, axis)
        resid = cond_l[k] * v_prev + cond_r[k] * v_next + via_b[k] * volts_a[slot_below[k]]
        resid = resid + via_a[k] * volts_a[slot_above[k]] + source[k] - diag[k] * v
        total = total + resid * resid
        drift = wind_r[k] * (v - v_next) - wind_l[k] * (v_prev - v)
        mr, ml = mob_r[k], mob_l[k]
        s = stress_in[layer[k]]
        s_prev, s_next = before(s, halo(STRESS, k, 0, 0), axis), after(s, halo(STRESS, k, 1, 0), axis)
        s = s + mr * (s_next - s) - ml * (s - s_prev) + drift
        stress_a[k] = s
        part = s + mr * (after(s, 0.0, axis) - s) - ml * (s - before(s, 0.0, axis)) + drift
        partial[k] = part
        weight[k] = drift
        put(STRESS1, k, [last(s, axis), last(part, axis)], [first(s, axis), first(part, axis)])
    start(STRESS1)

    def sum_copy(group, sem_s, sem_r, o, axis, sender):
        me, n = (gx, n_x) if axis == 0 else (gy, n_y)
        other = lax.rem(me + o, n)
        slot = me if sender else other
        return pltpu.make_async_remote_copy(
            src_ref=group.at[me], dst_ref=group.at[slot], send_sem=sem_s.at[o - 1], recv_sem=sem_r.at[slot],
            device_id=(other, gy) if axis == 0 else (gx, other), device_id_type=MESH,
        )

    def fold(a):
        r = a[0:8]
        for i in range(8, a.shape[0], 8):
            r = r + a[i:i + 8]
        out = r[:, 0:128]
        for j in range(128, a.shape[1], 128):
            out = out + r[:, j:j + 128]
        return out

    sum_x[gx] = fold(total)
    for o in range(1, n_x):
        sum_copy(sum_x, sx_send, sx_recv, o, 0, True).start()

    for l in range(layers):
        volts_fin[l] = volts_a[pos[l]]
    out_v = pltpu.make_async_copy(volts_fin, volts_out, out_sem.at[0])
    out_v.start()

    for o in range(1, n_x):
        sum_copy(sum_x, sx_send, sx_recv, o, 0, False).wait_recv()
    along = sum_x[0]
    for i in range(1, n_x):
        along = along + sum_x[i]
    sum_y[gy] = along
    for o in range(1, n_y):
        sum_copy(sum_y, sy_send, sy_recv, o, 1, True).start()

    arrive(STRESS1)
    for k in range(layers):
        axis = axis_of(k)
        mr, ml, s1 = mob_r[k], mob_l[k], stress_a[k]
        m_in, m_out = first(ml, axis), last(mr, axis)
        s_prev, s_next = halo(STRESS1, k, 0, 0), halo(STRESS1, k, 1, 0)
        s = partial[k] + jnp.where(is_first[axis], ml * s_prev, 0.0) + jnp.where(is_last[axis], mr * s_next, 0.0)
        h_prev = halo(STRESS1, k, 0, 1) + m_in * first(s1, axis)
        h_next = halo(STRESS1, k, 1, 1) + m_out * last(s1, axis)
        s = s + mr * (after(s, h_next, axis) - s) - ml * (s - before(s, h_prev, axis)) + weight[k]
        stress_a[k] = s
    for l in range(layers):
        stress_fin[l] = stress_a[pos[l]]
    out_s = pltpu.make_async_copy(stress_fin, stress_out, out_sem.at[1])
    out_s.start()

    for o in range(1, n_y):
        sum_copy(sum_y, sy_send, sy_recv, o, 1, False).wait_recv()
    whole = sum_y[0]
    for i in range(1, n_y):
        whole = whole + sum_y[i]
    nodes = layers * n_x * rows_x * n_y * rows_y
    mean = jnp.sum(whole, keepdims=True) * (1.0 / nodes)
    rms_out[0, 0] = jnp.sqrt(mean)[0, 0]

    for r in range(ROUNDS):
        for d in range(4):
            @pl.when(to_has[d])
            def _():
                edge_copy(r, d).wait_send()
    for o in range(1, n_x):
        sum_copy(sum_x, sx_send, sx_recv, o, 0, True).wait_send()
    for o in range(1, n_y):
        sum_copy(sum_y, sy_send, sy_recv, o, 1, True).wait_send()
    out_v.wait()
    out_s.wait()


def body(n_x, n_y, volts_start, seg_cond, via_cond, via_mask, pad_mask, load_current, stress_start, mobility, blocked, layer_dirs):
    layers, rows_x, rows_y = seg_cond.shape
    half = layers // 2
    f32, i32 = jnp.float32, jnp.int32
    full = (layers, rows_x, rows_y)
    vias = via_cond.shape
    flat = (rows_x, rows_y)
    dma = pltpu.SemaphoreType.DMA
    hbm = pl.BlockSpec(memory_space=pl.ANY)
    volts, stress, rms = pl.pallas_call(
        functools.partial(kernel, n_x, n_y, layers, rows_x, rows_y),
        out_shape=(
            jax.ShapeDtypeStruct(full, f32),
            jax.ShapeDtypeStruct(full, f32),
            jax.ShapeDtypeStruct((1, 1), f32),
        ),
        in_specs=[pl.BlockSpec(memory_space=pltpu.SMEM)] + [hbm] * 9,
        out_specs=(hbm, hbm, pl.BlockSpec(memory_space=pltpu.SMEM)),
        scratch_shapes=[
            pltpu.VMEM(full, f32), pltpu.VMEM(full, f32), pltpu.VMEM(vias, f32), pltpu.VMEM(vias, i32),
            pltpu.VMEM(flat, i32), pltpu.VMEM(flat, f32), pltpu.VMEM(full, f32), pltpu.VMEM(full, f32), pltpu.VMEM(full, i32),
        ]
        + [pltpu.VMEM(full, f32)] * 17
        + [
            pltpu.VMEM((ROUNDS, 2, 2, half, rows_y), f32), pltpu.VMEM((ROUNDS, 2, 2, half, rows_y), f32),
            pltpu.VMEM((ROUNDS, 2, half, rows_x, 128), f32), pltpu.VMEM((ROUNDS, 2, half, rows_x, 128), f32),
            pltpu.VMEM((n_x, 8, 128), f32), pltpu.VMEM((n_y, 8, 128), f32),
            dma((9,)), dma((2,)), dma((ROUNDS, 4)), dma((ROUNDS, 4)),
            dma((n_x,)), dma((n_x,)), dma((n_y,)), dma((n_y,)),
        ],
        compiler_params=pltpu.CompilerParams(
            collective_id=0, has_side_effects=True, vmem_limit_bytes=40 * 1024 * 1024
        ),
        cost_estimate=pl.CostEstimate(flops=20_000_000, bytes_accessed=5_000_000, transcendentals=0),
    )(layer_dirs, volts_start, seg_cond, via_cond, via_mask, pad_mask, load_current, stress_start, mobility, blocked)
    return volts, stress, rms.reshape(())


def solution(mesh):
    tile = P(None, "gx", "gy")
    flat = P("gx", "gy")
    in_specs = (tile, tile, tile, tile, flat, flat, tile, tile, tile, P())
    return jax.shard_map(
        functools.partial(body, mesh.shape["gx"], mesh.shape["gy"]),
        mesh=mesh, in_specs=in_specs, out_specs=(tile, tile, P()), check_vma=False,
    )
```

time: 179 us -> 40.2 us (0.22)
  starting transfers between devices: 88.1 us -> 0 us
  blocking collectives: 45.8 us -> 0 us
  Pallas kernels: 0 us -> 26.1 us
  waiting for transfers between devices: 19.9 us -> 0 us
  other arithmetic: 18.1 us -> 0 us
  local copies, waits for them, and re-layouts: 2.91 us -> 11.2 us
    ppermute x30 -> x0, starting transfers between devices: 88.1 us -> none  [the longest x14 63.3 us: with_halo(): lax.ppermute(tail, axis, [(i, (i + 1) % count) for i in range(ends)])]
    psum x1 -> x0, blocking collectives: 45.8 us -> none  [body(): squared = lax.psum(jnp.sum(resid * resid), ('gx', 'gy'))]
    pallas_call x0 -> x1, Pallas kernels: none -> 26.1 us  [body(): pl.pallas_call(functools.partial(kernel, n_x, n_y, layers, rows_x, rows_y...]
    ppermute x30 -> x0, waiting for transfers between devices: 19.9 us -> none  [the longest x14 15.2 us: with_halo(): lax.ppermute(head, axis, [((i + 1) % count, i) for i in range(ends)])]
    add x6 -> x0, other arithmetic: 11.1 us -> none  [the longest x3 8.37 us: body(): stress + mobile_x * (side[:, 2:, 1:-1] - stress)]
    unnamed x36 -> x22, local copies, waits for them, and re-layouts: 0.73 us -> 11.2 us
    slice x7 -> x0, other arithmetic: 2.67 us -> none  [the longest x4 2.35 us: with_halo(): head = lax.slice_in_dim(cells, 0, width, axis=dim)]
    reduce_sum x1 -> x0, other arithmetic: 2.4 us -> none  [body(): squared = lax.psum(jnp.sum(resid * resid), ('gx', 'gy'))]
  transfers between devices with their start and end apart: 30 -> 0, of which waited for: 10 -> 0; matrix products, arithmetic and copies ran while one was open for 4% -> 0% of each run, Pallas kernels for 0% -> 0%
where the time goes in v1:
time: 40.2 us; the launch traced here: 39.7 us
  Pallas kernels  26.1 us (65%)
  local copies, waits for them, and re-layouts  11.2 us (28%)
  between operations  2.42 us (6%)
    pallas_call x1, Pallas kernels, body(): pl.pallas_call(functools.partial(kernel, n_x, n_y, layers, rows_x, rows_y...  26.1 us
    unnamed x22, local copies, waits for them, and re-layouts  11.2 us

profile of v1, /device:TPU:0, one launch (start us, length us, event | category | flops | bytes accessed | tf_op | source)
XLA Modules:
  0.0 39.7 jit_solution(16855505988620557312)
XLA Ops:
  0.6 0.0 copy-start
  0.6 1.0 %copy-done = f32[8,16,1024]{2,1,0:T(8,128)S(1)} copy-done((f32[8,16,1024]{2,1,0:T(8,128)S(1)}, f32[8,16,1024]{2,1,0:T(8,128)}, u32[]{:S(2)}) %copy-start) | copy-done | bytes 524312
  1.7 0.0 copy-start.1
  1.7 1.0 %copy-done.1 = f32[8,16,1024]{2,1,0:T(8,128)S(1)} copy-done((f32[8,16,1024]{2,1,0:T(8,128)S(1)}, f32[8,16,1024]{2,1,0:T(8,128)}, u32[]{:S(2)}) %copy-start.1) | copy-done | bytes 524312
  2.7 0.0 copy-start.2
  2.7 1.0 %copy-done.2 = f32[8,16,1024]{2,1,0:T(8,128)S(1)} copy-done((f32[8,16,1024]{2,1,0:T(8,128)S(1)}, f32[8,16,1024]{2,1,0:T(8,128)}, u32[]{:S(2)}) %copy-start.2) | copy-done | bytes 524312
  3.8 0.0 copy-start.3
  3.8 1.0 %copy-done.3 = f32[8,16,1024]{2,1,0:T(8,128)S(1)} copy-done((f32[8,16,1024]{2,1,0:T(8,128)S(1)}, f32[8,16,1024]{2,1,0:T(8,128)}, u32[]{:S(2)}) %copy-start.3) | copy-done | bytes 524312
  4.8 0.0 copy-start.4
  4.8 1.0 %copy-done.4 = s32[8,16,1024]{2,1,0:T(8,128)S(1)} copy-done((s32[8,16,1024]{2,1,0:T(8,128)S(1)}, s32[8,16,1024]{2,1,0:T(8,128)}, u32[]{:S(2)}) %copy-start.4) | copy-done | bytes 524312
  5.8 0.0 copy-start.5
  5.8 1.0 %copy-done.5 = f32[7,16,1024]{2,1,0:T(8,128)S(1)} copy-done((f32[7,16,1024]{2,1,0:T(8,128)S(1)}, f32[7,16,1024]{2,1,0:T(8,128)}, u32[]{:S(2)}) %copy-start.5) | copy-done | bytes 458776
  6.9 0.0 copy-start.6
  6.9 1.0 %copy-done.6 = s32[7,16,1024]{2,1,0:T(8,128)S(1)} copy-done((s32[7,16,1024]{2,1,0:T(8,128)S(1)}, s32[7,16,1024]{2,1,0:T(8,128)}, u32[]{:S(2)}) %copy-start.6) | copy-done | bytes 458776
  7.9 0.0 copy-start.7
  7.9 0.8 %copy-done.7 = s32[16,1024]{1,0:T(8,128)S(1)} copy-done((s32[16,1024]{1,0:T(8,128)S(1)}, s32[16,1024]{1,0:T(8,128)}, u32[]{:S(2)}) %copy-start.7) | copy-done | bytes 65560
  8.7 0.0 copy-start.8
  8.7 0.8 %copy-done.8 = f32[16,1024]{1,0:T(8,128)S(1)} copy-done((f32[16,1024]{1,0:T(8,128)S(1)}, f32[16,1024]{1,0:T(8,128)}, u32[]{:S(2)}) %copy-start.8) | copy-done | bytes 65560
  9.6 0.0 copy-start.9
  9.6 0.7 %copy-done.9 = s32[8]{0:T(128)S(1)} copy-done((s32[8]{0:T(128)S(1)}, s32[8]{0:T(128)}, u32[]{:S(2)}) %copy-start.9) | copy-done | bytes 56
  10.2 26.1 %shard_map.121 = (f32[8,16,1024]{2,1,0:T(8,128)S(1)}, f32[8,16,1024]{2,1,0:T(8,128)S(1)}, f32[1,1]{1,0:T(1,128)}) custom-call(s32[8]{0:T(128)S(1)} %copy-done.9, f32[8,16,1024]{2,1,0:T(8,128)S(1)} %copy-done, f32[8,16,1024]{2,1,0:T(8,128)S(1)} %copy-done.1, f32[7,16,1024]{2,1,0:T(8,128)S(1)} %copy-done.5, s32[7,16,1024]{2,1,0:T(8,128)S(1)} %copy-done.6, ...), custom_call_target="tpu_custom_call" | custom-call | flops 20000000 | bytes 5000000 | tf_op jit(solution)/shard_map/pallas_call | solution.py:370
  36.3 0.8 %copy.16 = f32[8,16,1024]{2,1,0:T(8,128)} copy(f32[8,16,1024]{2,1,0:T(8,128)S(1)} %get-tuple-element.12) | data formatting | bytes 1048576
  37.1 0.8 %copy.17 = f32[8,16,1024]{2,1,0:T(8,128)} copy(f32[8,16,1024]{2,1,0:T(8,128)S(1)} %get-tuple-element.13) | data formatting | bytes 1048576
Async XLA Ops:
  0.6 1.0 %copy-start = (f32[8,16,1024]{2,1,0:T(8,128)S(1)}, f32[8,16,1024]{2,1,0:T(8,128)}, u32[]{:S(2)}) copy-start(f32[8,16,1024]{2,1,0:T(8,128)} %volts_hbm.1) | copy-start | bytes 1572868
  1.7 1.0 %copy-start.1 = (f32[8,16,1024]{2,1,0:T(8,128)S(1)}, f32[8,16,1024]{2,1,0:T(8,128)}, u32[]{:S(2)}) copy-start(f32[8,16,1024]{2,1,0:T(8,128)} %seg_hbm.1) | copy-start | bytes 1572868
  2.7 1.0 %copy-start.2 = (f32[8,16,1024]{2,1,0:T(8,128)S(1)}, f32[8,16,1024]{2,1,0:T(8,128)}, u32[]{:S(2)}) copy-start(f32[8,16,1024]{2,1,0:T(8,128)} %stress_hbm.1) | copy-start | bytes 1572868
  3.8 1.0 %copy-start.3 = (f32[8,16,1024]{2,1,0:T(8,128)S(1)}, f32[8,16,1024]{2,1,0:T(8,128)}, u32[]{:S(2)}) copy-start(f32[8,16,1024]{2,1,0:T(8,128)} %mob_hbm.1) | copy-start | bytes 1572868
  4.8 1.0 %copy-start.4 = (s32[8,16,1024]{2,1,0:T(8,128)S(1)}, s32[8,16,1024]{2,1,0:T(8,128)}, u32[]{:S(2)}) copy-start(s32[8,16,1024]{2,1,0:T(8,128)} %blk_hbm.1) | copy-start | bytes 1572868
  5.8 1.0 %copy-start.5 = (f32[7,16,1024]{2,1,0:T(8,128)S(1)}, f32[7,16,1024]{2,1,0:T(8,128)}, u32[]{:S(2)}) copy-start(f32[7,16,1024]{2,1,0:T(8,128)} %via_hbm.1) | copy-start | bytes 1376260
  6.9 1.0 %copy-start.6 = (s32[7,16,1024]{2,1,0:T(8,128)S(1)}, s32[7,16,1024]{2,1,0:T(8,128)}, u32[]{:S(2)}) copy-start(s32[7,16,1024]{2,1,0:T(8,128)} %vmask_hbm.1) | copy-start | bytes 1376260
  7.9 0.8 %copy-start.7 = (s32[16,1024]{1,0:T(8,128)S(1)}, s32[16,1024]{1,0:T(8,128)}, u32[]{:S(2)}) copy-start(s32[16,1024]{1,0:T(8,128)} %pad_hbm.1) | copy-start | bytes 196612
  8.7 0.8 %copy-start.8 = (f32[16,1024]{1,0:T(8,128)S(1)}, f32[16,1024]{1,0:T(8,128)}, u32[]{:S(2)}) copy-start(f32[16,1024]{1,0:T(8,128)} %load_hbm.1) | copy-start | bytes 196612
  9.6 0.7 %copy-start.9 = (s32[8]{0:T(128)S(1)}, s32[8]{0:T(128)}, u32[]{:S(2)}) copy-start(s32[8]{0:T(128)} %dirs.1) | copy-start | bytes 100

commit v2 on v1

--- a/solution.py
+++ b/solution.py
@@ -18,9 +18,9 @@
 
 def kernel(
     n_x, n_y, layers, rows_x, rows_y,
-    dirs, volts_hbm, seg_hbm, via_hbm, vmask_hbm, pad_hbm, load_hbm, stress_hbm, mob_hbm, blk_hbm,
+    dirs_hbm, volts_hbm, seg_hbm, via_hbm, vmask_hbm, pad_hbm, load_hbm, stress_hbm, mob_hbm, blk_hbm,
     volts_out, stress_out, rms_out,
-    volts_in, seg_in, via_in, vmask_in, pad_in, load_in, stress_in, mob_in, blk_in,
+    dirs, volts_in, seg_in, via_in, vmask_in, pad_in, load_in, stress_in, mob_in, blk_in,
     cond_r, cond_l, via_b, via_a, source, diag, weight, partial,
     mob_r, mob_l, wind_r, wind_l, volts_a, volts_b, stress_a, volts_fin, stress_fin,
     send_x, recv_x, send_y, recv_y, sum_x, sum_y,
@@ -35,11 +35,12 @@
         for i, (src, dst) in enumerate(
             [
                 (volts_hbm, volts_in), (seg_hbm, seg_in), (via_hbm, via_in), (vmask_hbm, vmask_in), (pad_hbm, pad_in),
-                (load_hbm, load_in), (stress_hbm, stress_in), (mob_hbm, mob_in), (blk_hbm, blk_in),
+                (load_hbm, load_in), (stress_hbm, stress_in), (mob_hbm, mob_in), (blk_hbm, blk_in), (dirs_hbm, dirs),
             ]
         )
     ]
-    for move in moves:
+    moves[9].start()
+    for move in moves[:9]:
         move.start()
 
     barrier = pltpu.get_barrier_semaphore()
@@ -66,8 +67,8 @@
             device_id=target[d], device_id_type=MESH,
         )
 
-    def start(r):
-        for d in range(4):
+    def start(r, axis):
+        for d in (2 * axis, 2 * axis + 1):
             @pl.when(to_has[d])
             def _():
                 edge_copy(r, d).start()
@@ -89,6 +90,7 @@
             for r in range(ROUNDS):
                 recv_y[r, d] = jnp.full(recv_y.shape[2:], 1.0 if r == PARTIAL else 0.0, jnp.float32)
 
+    moves[9].wait()
     is_y = [dirs[l] for l in range(layers)]
     pos = []
     seen_x, seen_y = jnp.int32(0), jnp.int32(half)
@@ -165,8 +167,10 @@
         cond_l[k] = before(cr, 0.0, axis)
         v = volts_in[layer[k]]
         put(VOLTS, k, [last(v, axis), last(cr, axis)], [first(v, axis)])
-    pl.semaphore_wait(barrier, n_x + n_y - 2)
-    start(VOLTS)
+        if k == half - 1:
+            pl.semaphore_wait(barrier, n_x + n_y - 2)
+            start(VOLTS, 0)
+    start(VOLTS, 1)
 
     for move in moves[2:6]:
         move.wait()
@@ -190,9 +194,11 @@
         diag[k] = dg
         partial[k] = num
         put(PARTIAL, k, [last(num, axis), last(dg, axis)], [first(num, axis), first(dg, axis)])
-    start(PARTIAL)
-
-    for move in moves[6:]:
+        if k == half - 1:
+            start(PARTIAL, 0)
+    start(PARTIAL, 1)
+
+    for move in moves[6:9]:
         move.wait()
     for k in range(layers):
         axis = axis_of(k)
@@ -201,7 +207,9 @@
         mob_r[k] = mr
         s = stress_in[l]
         put(STRESS, k, [last(s, axis), last(mr, axis)], [first(s, axis)])
-    start(STRESS)
+        if k == half - 1:
+            start(STRESS, 0)
+    start(STRESS, 1)
 
     def edge_next(k, v_prev, n_prev, v_next, n_next, v):
         axis = axis_of(k)
@@ -243,7 +251,9 @@
         num = inflow(volts_b, k, v, 0.0, 0.0)
         partial[k] = num
         put(VOLTS2, k, [last(v, axis), last(num, axis)], [first(v, axis), first(num, axis)])
-    start(VOLTS2)
+        if k == half - 1:
+            start(VOLTS2, 0)
+    start(VOLTS2, 1)
 
     arrive(STRESS)
     for k in range(layers):
@@ -282,7 +292,9 @@
         partial[k] = part
         weight[k] = drift
         put(STRESS1, k, [last(s, axis), last(part, axis)], [first(s, axis), first(part, axis)])
-    start(STRESS1)
+        if k == half - 1:
+            start(STRESS1, 0)
+    start(STRESS1, 1)
 
     def sum_copy(group, sem_s, sem_r, o, axis, sender):
         me, n = (gx, n_x) if axis == 0 else (gy, n_y)
@@ -366,7 +378,11 @@
     vias = via_cond.shape
     flat = (rows_x, rows_y)
     dma = pltpu.SemaphoreType.DMA
-    hbm = pl.BlockSpec(memory_space=pl.ANY)
+    out = pl.BlockSpec(memory_space=pl.ANY)
+    hbm = pl.BlockSpec(memory_space=pltpu.HBM)
+    operands = (
+        layer_dirs, volts_start, seg_cond, via_cond, via_mask, pad_mask, load_current, stress_start, mobility, blocked
+    )
     volts, stress, rms = pl.pallas_call(
         functools.partial(kernel, n_x, n_y, layers, rows_x, rows_y),
         out_shape=(
@@ -374,9 +390,10 @@
             jax.ShapeDtypeStruct(full, f32),
             jax.ShapeDtypeStruct((1, 1), f32),
         ),
-        in_specs=[pl.BlockSpec(memory_space=pltpu.SMEM)] + [hbm] * 9,
-        out_specs=(hbm, hbm, pl.BlockSpec(memory_space=pltpu.SMEM)),
+        in_specs=[hbm] * 10,
+        out_specs=(out, out, pl.BlockSpec(memory_space=pltpu.SMEM)),
         scratch_shapes=[
+            pltpu.SMEM((layers,), i32),
             pltpu.VMEM(full, f32), pltpu.VMEM(full, f32), pltpu.VMEM(vias, f32), pltpu.VMEM(vias, i32),
             pltpu.VMEM(flat, i32), pltpu.VMEM(flat, f32), pltpu.VMEM(full, f32), pltpu.VMEM(full, f32), pltpu.VMEM(full, i32),
         ]
@@ -385,14 +402,14 @@
             pltpu.VMEM((ROUNDS, 2, 2, half, rows_y), f32), pltpu.VMEM((ROUNDS, 2, 2, half, rows_y), f32),
             pltpu.VMEM((ROUNDS, 2, half, rows_x, 128), f32), pltpu.VMEM((ROUNDS, 2, half, rows_x, 128), f32),
             pltpu.VMEM((n_x, 8, 128), f32), pltpu.VMEM((n_y, 8, 128), f32),
-            dma((9,)), dma((2,)), dma((ROUNDS, 4)), dma((ROUNDS, 4)),
+            dma((10,)), dma((2,)), dma((ROUNDS, 4)), dma((ROUNDS, 4)),
             dma((n_x,)), dma((n_x,)), dma((n_y,)), dma((n_y,)),
         ],
         compiler_params=pltpu.CompilerParams(
             collective_id=0, has_side_effects=True, vmem_limit_bytes=40 * 1024 * 1024
         ),
         cost_estimate=pl.CostEstimate(flops=20_000_000, bytes_accessed=5_000_000, transcendentals=0),
-    )(layer_dirs, volts_start, seg_cond, via_cond, via_mask, pad_mask, load_current, stress_start, mobility, blocked)
+    )(*[pltpu.with_memory_space_constraint(operand, pltpu.HBM) for operand in operands])
     return volts, stress, rms.reshape(())
 
 

time: 40.2 us -> 28.1 us (0.70)
  local copies, waits for them, and re-layouts: 11.2 us -> 1.59 us
  Pallas kernels: 26.1 us -> 24 us
    unnamed x22 -> x2, local copies, waits for them, and re-layouts: 11.2 us -> 1.59 us
    pallas_call x1, Pallas kernels: 26.1 us -> 24 us  [body(): pl.pallas_call(functools.partial(kernel, n_x, n_y, layers, rows_x, rows_y...]
where the time goes in v2:
time: 28.1 us; the launch traced here: 27.9 us
  Pallas kernels  24 us (85%)
  between operations  2.33 us (8%)
  local copies, waits for them, and re-layouts  1.59 us (6%)
    pallas_call x1, Pallas kernels, body(): pl.pallas_call(functools.partial(kernel, n_x, n_y, layers, rows_x, rows_y...  24 us
    unnamed x2, local copies, waits for them, and re-layouts  1.59 us

profile of v2, /device:TPU:0, one launch (start us, length us, event | category | flops | bytes accessed | tf_op | source)
XLA Modules:
  0.0 27.9 jit_solution(5605752698519834359)
XLA Ops:
  0.6 24.0 %shard_map.121 = (f32[8,16,1024]{2,1,0:T(8,128)S(1)}, f32[8,16,1024]{2,1,0:T(8,128)S(1)}, f32[1,1]{1,0:T(1,128)}) custom-call(s32[8]{0:T(128)} %dirs_hbm.1, f32[8,16,1024]{2,1,0:T(8,128)} %volts_hbm.1, f32[8,16,1024]{2,1,0:T(8,128)} %seg_hbm.1, f32[7,16,1024]{2,1,0:T(8,128)} %via_hbm.1, s32[7,16,1024]{2,1,0:T(8,128)} %vmask_hbm.1, s32[16,1024]{1,0:T(8,128)} %pad_hbm.1, ...), custom_call_target="tpu_custom_call" | custom-call | flops 20000000 | bytes 5000000 | tf_op jit(solution)/shard_map/pallas_call | solution.py:386
  24.7 0.8 %copy.16 = f32[8,16,1024]{2,1,0:T(8,128)} copy(f32[8,16,1024]{2,1,0:T(8,128)S(1)} %get-tuple-element.12) | data formatting | bytes 1048576
  25.5 0.8 %copy.17 = f32[8,16,1024]{2,1,0:T(8,128)} copy(f32[8,16,1024]{2,1,0:T(8,128)S(1)} %get-tuple-element.13) | data formatting | bytes 1048576

commit v3 on v2

--- a/solution.py
+++ b/solution.py
@@ -21,8 +21,8 @@
     dirs_hbm, volts_hbm, seg_hbm, via_hbm, vmask_hbm, pad_hbm, load_hbm, stress_hbm, mob_hbm, blk_hbm,
     volts_out, stress_out, rms_out,
     dirs, volts_in, seg_in, via_in, vmask_in, pad_in, load_in, stress_in, mob_in, blk_in,
-    cond_r, cond_l, via_b, via_a, source, diag, weight, partial,
-    mob_r, mob_l, wind_r, wind_l, volts_a, volts_b, stress_a, volts_fin, stress_fin,
+    cond, via_b, via_a, source, anchor, diag, weight, partial, mob, volts_a, volts_b, stress_a, stress_b,
+    volts_fin, stress_fin,
     send_x, recv_x, send_y, recv_y, sum_x, sum_y,
     in_sem, out_sem, send_sem, recv_sem, sx_send, sx_recv, sy_send, sy_recv,
 ):
@@ -163,14 +163,24 @@
     for k in range(layers):
         axis = axis_of(k)
         cr = jnp.where(outer[axis], 0.0, seg_in[layer[k]])
-        cond_r[k] = cr
-        cond_l[k] = before(cr, 0.0, axis)
+        cond[k] = cr
         v = volts_in[layer[k]]
         put(VOLTS, k, [last(v, axis), last(cr, axis)], [first(v, axis)])
         if k == half - 1:
             pl.semaphore_wait(barrier, n_x + n_y - 2)
             start(VOLTS, 0)
     start(VOLTS, 1)
+
+    def inside(k, coef, field, minus=None):
+        axis = axis_of(k)
+        flux = coef * (pltpu.roll(field, length[axis] - 1, axis) - field)
+        if minus is not None:
+            flux = flux - minus
+        flux = jnp.where(is_last[axis], 0.0, flux)
+        return flux - pltpu.roll(flux, 1, axis)
+
+    def upright(k, v, v_below, v_above):
+        return via_b[k] * v_below + via_a[k] * v_above + source[k] - anchor[k] * v
 
     for move in moves[2:6]:
         move.wait()
@@ -180,20 +190,22 @@
         axis = axis_of(k)
         l = layer[k]
         up = jnp.minimum(l, layers - 2)
-        va = via_in[up] * vmask_in[up].astype(jnp.float32) * jnp.where(l < layers - 1, 1.0, 0.0)
-        vb = via_in[below[k]] * vmask_in[below[k]].astype(jnp.float32) * jnp.where(l > 0, 1.0, 0.0)
+        va = via_in[up] * (vmask_in[up].astype(jnp.float32) * jnp.where(l < layers - 1, 1.0, 0.0))
+        vb = via_in[below[k]] * (vmask_in[below[k]].astype(jnp.float32) * jnp.where(l > 0, 1.0, 0.0))
         top = pads * jnp.where(l == layers - 1, 1.0, 0.0)
         src = top * supply_volts - load * jnp.where(l == 0, 1.0, 0.0)
+        hold = va + vb + top
         via_a[k] = va
         via_b[k] = vb
         source[k] = src
+        anchor[k] = hold
         v = volts_in[l]
-        cl, cr = cond_l[k], cond_r[k]
-        dg = cl + cr + va + vb + top
-        num = cl * before(v, 0.0, axis) + cr * after(v, 0.0, axis) + vb * volts_in[below[k]] + va * volts_in[above[k]] + src
+        cr = cond[k]
+        dg = hold + cr + before(cr, 0.0, axis)
+        res = inside(k, cr, v) + vb * volts_in[below[k]] + va * volts_in[above[k]] + src - hold * v
         diag[k] = dg
-        partial[k] = num
-        put(PARTIAL, k, [last(num, axis), last(dg, axis)], [first(num, axis), first(dg, axis)])
+        partial[k] = res
+        put(PARTIAL, k, [last(res, axis), last(dg, axis)], [first(res, axis), first(dg, axis)])
         if k == half - 1:
             start(PARTIAL, 0)
     start(PARTIAL, 1)
@@ -204,53 +216,52 @@
         axis = axis_of(k)
         l = layer[k]
         mr = jnp.where(outer[axis], 0.0, mob_in[l] * (1.0 - blk_in[l].astype(jnp.float32)))
-        mob_r[k] = mr
+        mob[k] = mr
         s = stress_in[l]
         put(STRESS, k, [last(s, axis), last(mr, axis)], [first(s, axis)])
         if k == half - 1:
             start(STRESS, 0)
     start(STRESS, 1)
 
-    def edge_next(k, v_prev, n_prev, v_next, n_next, v):
-        axis = axis_of(k)
-        c_in, c_out = halo(VOLTS, k, 0, 1), last(cond_r[k], axis)
-        h_prev = (1.0 - damping) * v_prev + damping * (n_prev + c_in * first(v, axis)) / halo(PARTIAL, k, 0, 1)
-        h_next = (1.0 - damping) * v_next + damping * (n_next + c_out * last(v, axis)) / (halo(PARTIAL, k, 1, 1) + c_out)
+    def edge_next(k, v_prev, r_prev, v_next, r_next, v):
+        axis = axis_of(k)
+        c_in, c_out = halo(VOLTS, k, 0, 1), last(cond[k], axis)
+        h_prev = v_prev + damping * (r_prev + c_in * (first(v, axis) - v_prev)) / halo(PARTIAL, k, 0, 1)
+        h_next = v_next + damping * (r_next + c_out * (last(v, axis) - v_next)) / (halo(PARTIAL, k, 1, 1) + c_out)
         return h_prev, h_next
 
+    def edges(axis, at_first, at_last):
+        return jnp.where(is_first[axis], at_first, jnp.where(is_last[axis], at_last, 0.0))
+
     arrive(VOLTS)
     for k in range(layers):
         axis = axis_of(k)
-        c_in = halo(VOLTS, k, 0, 1)
-        cl = jnp.where(is_first[axis], c_in, cond_l[k])
-        cond_l[k] = cl
-        dg = diag[k] + jnp.where(is_first[axis], c_in, 0.0)
-        diag[k] = dg
-        w = damping / dg
+        c_in, c_out = halo(VOLTS, k, 0, 1), last(cond[k], axis)
+        v = volts_in[layer[k]]
+        w = damping / (diag[k] + jnp.where(is_first[axis], c_in, 0.0))
         weight[k] = w
-        num = partial[k] + jnp.where(is_first[axis], c_in * halo(VOLTS, k, 0, 0), 0.0)
-        num = num + jnp.where(is_last[axis], cond_r[k] * halo(VOLTS, k, 1, 0), 0.0)
-        volts_a[k] = (1.0 - damping) * volts_in[layer[k]] + w * num
-
-    def inflow(v_ref, k, v, h_prev, h_next):
-        axis = axis_of(k)
-        lateral = cond_l[k] * before(v, h_prev, axis) + cond_r[k] * after(v, h_next, axis)
-        return lateral + via_b[k] * v_ref[slot_below[k]] + via_a[k] * v_ref[slot_above[k]] + source[k]
+        cross = edges(
+            axis, c_in * (halo(VOLTS, k, 0, 0) - first(v, axis)), c_out * (halo(VOLTS, k, 1, 0) - last(v, axis))
+        )
+        volts_a[k] = v + w * (partial[k] + cross)
 
     arrive(PARTIAL)
     for k in range(layers):
+        axis = axis_of(k)
         v = volts_a[k]
         h_prev, h_next = edge_next(
             k, halo(VOLTS, k, 0, 0), halo(PARTIAL, k, 0, 0), halo(VOLTS, k, 1, 0), halo(PARTIAL, k, 1, 0),
             volts_in[layer[k]],
         )
-        volts_b[k] = (1.0 - damping) * v + weight[k] * inflow(volts_a, k, v, h_prev, h_next)
+        flux = cond[k] * (after(v, h_next, axis) - v)
+        net = flux - before(flux, halo(VOLTS, k, 0, 1) * (first(v, axis) - h_prev), axis)
+        volts_b[k] = v + weight[k] * (net + upright(k, v, volts_a[slot_below[k]], volts_a[slot_above[k]]))
     for k in range(layers):
         axis = axis_of(k)
         v = volts_b[k]
-        num = inflow(volts_b, k, v, 0.0, 0.0)
-        partial[k] = num
-        put(VOLTS2, k, [last(v, axis), last(num, axis)], [first(v, axis), first(num, axis)])
+        res = inside(k, cond[k], v) + upright(k, v, volts_b[slot_below[k]], volts_b[slot_above[k]])
+        volts_a[k] = v + weight[k] * res
+        put(VOLTS2, k, [last(v, axis), last(res, axis)], [first(v, axis), first(res, axis)])
         if k == half - 1:
             start(VOLTS2, 0)
     start(VOLTS2, 1)
@@ -258,43 +269,45 @@
     arrive(STRESS)
     for k in range(layers):
         axis = axis_of(k)
-        mr = mob_r[k]
-        ml = before(mr, halo(STRESS, k, 0, 1), axis)
-        mob_l[k] = ml
-        wind_r[k] = wind_factor * mr * cond_r[k]
-        wind_l[k] = wind_factor * ml * cond_l[k]
+        s = stress_in[layer[k]]
+        flux = mob[k] * (after(s, halo(STRESS, k, 1, 0), axis) - s)
+        at_first = halo(STRESS, k, 0, 1) * (first(s, axis) - halo(STRESS, k, 0, 0))
+        stress_a[k] = s + flux - before(flux, at_first, axis)
 
     arrive(VOLTS2)
-    for k in range(layers):
-        axis = axis_of(k)
-        num = partial[k] + jnp.where(is_first[axis], cond_l[k] * halo(VOLTS2, k, 0, 0), 0.0)
-        num = num + jnp.where(is_last[axis], cond_r[k] * halo(VOLTS2, k, 1, 0), 0.0)
-        volts_a[k] = (1.0 - damping) * volts_b[k] + weight[k] * num
-
-    total = jnp.zeros(shape, jnp.float32)
-    for k in range(layers):
-        axis = axis_of(k)
-        v = volts_a[k]
-        h_prev, h_next = edge_next(
-            k, halo(VOLTS2, k, 0, 0), halo(VOLTS2, k, 0, 1), halo(VOLTS2, k, 1, 0), halo(VOLTS2, k, 1, 1), volts_b[k]
-        )
-        v_prev, v_next = before(v, h_prev, axis), after(v, h_next, axis)
-        resid = cond_l[k] * v_prev + cond_r[k] * v_next + via_b[k] * volts_a[slot_below[k]]
-        resid = resid + via_a[k] * volts_a[slot_above[k]] + source[k] - diag[k] * v
-        total = total + resid * resid
-        drift = wind_r[k] * (v - v_next) - wind_l[k] * (v_prev - v)
-        mr, ml = mob_r[k], mob_l[k]
-        s = stress_in[layer[k]]
-        s_prev, s_next = before(s, halo(STRESS, k, 0, 0), axis), after(s, halo(STRESS, k, 1, 0), axis)
-        s = s + mr * (s_next - s) - ml * (s - s_prev) + drift
+    entry, pull = [], []
+    for k in range(layers):
+        axis = axis_of(k)
+        c_in, c_out = halo(VOLTS, k, 0, 1), last(cond[k], axis)
+        v_prev, v_next, v = halo(VOLTS2, k, 0, 0), halo(VOLTS2, k, 1, 0), volts_b[k]
+        h_prev, h_next = edge_next(k, v_prev, halo(VOLTS2, k, 0, 1), v_next, halo(VOLTS2, k, 1, 1), v)
+        cross = edges(axis, c_in * (v_prev - first(v, axis)), c_out * (v_next - last(v, axis)))
+        v = volts_a[k] + weight[k] * cross
+        volts_a[k] = v
+        flux = cond[k] * (after(v, h_next, axis) - v)
+        partial[k] = flux
+        at_first = c_in * (first(v, axis) - h_prev)
+        mr = mob[k]
+        wind = wind_factor * mr * flux
+        diag[k] = wind
+        wind_first = wind_factor * halo(STRESS, k, 0, 1) * at_first
+        entry.append(at_first)
+        pull.append(wind_first)
+        s = stress_a[k] - wind + before(wind, wind_first, axis)
         stress_a[k] = s
-        part = s + mr * (after(s, 0.0, axis) - s) - ml * (s - before(s, 0.0, axis)) + drift
-        partial[k] = part
-        weight[k] = drift
+        part = s + inside(k, mr, s, wind)
+        stress_b[k] = part
         put(STRESS1, k, [last(s, axis), last(part, axis)], [first(s, axis), first(part, axis)])
         if k == half - 1:
             start(STRESS1, 0)
     start(STRESS1, 1)
+
+    total = jnp.zeros(shape, jnp.float32)
+    for k in range(layers):
+        flux = partial[k]
+        net = flux - before(flux, entry[k], axis_of(k))
+        res = net + upright(k, volts_a[k], volts_a[slot_below[k]], volts_a[slot_above[k]])
+        total = total + res * res
 
     def sum_copy(group, sem_s, sem_r, o, axis, sender):
         me, n = (gx, n_x) if axis == 0 else (gy, n_y)
@@ -323,26 +336,28 @@
     out_v = pltpu.make_async_copy(volts_fin, volts_out, out_sem.at[0])
     out_v.start()
 
-    for o in range(1, n_x):
-        sum_copy(sum_x, sx_send, sx_recv, o, 0, False).wait_recv()
-    along = sum_x[0]
-    for i in range(1, n_x):
-        along = along + sum_x[i]
-    sum_y[gy] = along
-    for o in range(1, n_y):
-        sum_copy(sum_y, sy_send, sy_recv, o, 1, True).start()
-
     arrive(STRESS1)
     for k in range(layers):
         axis = axis_of(k)
-        mr, ml, s1 = mob_r[k], mob_l[k], stress_a[k]
-        m_in, m_out = first(ml, axis), last(mr, axis)
+        mr, wind, s = mob[k], diag[k], stress_a[k]
+        m_in, m_out = halo(STRESS, k, 0, 1), last(mr, axis)
         s_prev, s_next = halo(STRESS1, k, 0, 0), halo(STRESS1, k, 1, 0)
-        s = partial[k] + jnp.where(is_first[axis], ml * s_prev, 0.0) + jnp.where(is_last[axis], mr * s_next, 0.0)
-        h_prev = halo(STRESS1, k, 0, 1) + m_in * first(s1, axis)
-        h_next = halo(STRESS1, k, 1, 1) + m_out * last(s1, axis)
-        s = s + mr * (after(s, h_next, axis) - s) - ml * (s - before(s, h_prev, axis)) + weight[k]
-        stress_a[k] = s
+        flux_in = m_in * (first(s, axis) - s_prev) - pull[k]
+        flux_out = m_out * (s_next - last(s, axis)) - last(wind, axis)
+        s = stress_b[k] + edges(axis, -flux_in, flux_out)
+        h_prev = halo(STRESS1, k, 0, 1) + flux_in
+        h_next = halo(STRESS1, k, 1, 1) - flux_out
+        flux = mr * (after(s, h_next, axis) - s) - wind
+        stress_a[k] = s + flux - before(flux, m_in * (first(s, axis) - h_prev) - pull[k], axis)
+        if k == half - 1:
+            for o in range(1, n_x):
+                sum_copy(sum_x, sx_send, sx_recv, o, 0, False).wait_recv()
+            along = sum_x[0]
+            for i in range(1, n_x):
+                along = along + sum_x[i]
+            sum_y[gy] = along
+            for o in range(1, n_y):
+                sum_copy(sum_y, sy_send, sy_recv, o, 1, True).start()
     for l in range(layers):
         stress_fin[l] = stress_a[pos[l]]
     out_s = pltpu.make_async_copy(stress_fin, stress_out, out_sem.at[1])
@@ -368,6 +383,20 @@
         sum_copy(sum_y, sy_send, sy_recv, o, 1, True).wait_send()
     out_v.wait()
     out_s.wait()
+
+
+def deliver(volts_ref, stress_ref, volts_out, stress_out, sems):
+    parts = sems.shape[1]
+    count = volts_ref.shape[0] // parts
+    moves = [
+        pltpu.make_async_copy(src.at[i * count:(i + 1) * count], dst.at[i * count:(i + 1) * count], sems.at[j, i])
+        for j, (src, dst) in enumerate([(volts_ref, volts_out), (stress_ref, stress_out)])
+        for i in range(parts)
+    ]
+    for move in moves:
+        move.start()
+    for move in moves:
+        move.wait()
 
 
 def body(n_x, n_y, volts_start, seg_cond, via_cond, via_mask, pad_mask, load_current, stress_start, mobility, blocked, layer_dirs):
@@ -397,7 +426,7 @@
             pltpu.VMEM(full, f32), pltpu.VMEM(full, f32), pltpu.VMEM(vias, f32), pltpu.VMEM(vias, i32),
             pltpu.VMEM(flat, i32), pltpu.VMEM(flat, f32), pltpu.VMEM(full, f32), pltpu.VMEM(full, f32), pltpu.VMEM(full, i32),
         ]
-        + [pltpu.VMEM(full, f32)] * 17
+        + [pltpu.VMEM(full, f32)] * 15
         + [
             pltpu.VMEM((ROUNDS, 2, 2, half, rows_y), f32), pltpu.VMEM((ROUNDS, 2, 2, half, rows_y), f32),
             pltpu.VMEM((ROUNDS, 2, half, rows_x, 128), f32), pltpu.VMEM((ROUNDS, 2, half, rows_x, 128), f32),
@@ -410,6 +439,14 @@
         ),
         cost_estimate=pl.CostEstimate(flops=20_000_000, bytes_accessed=5_000_000, transcendentals=0),
     )(*[pltpu.with_memory_space_constraint(operand, pltpu.HBM) for operand in operands])
+    volts, stress = pl.pallas_call(
+        deliver,
+        out_shape=(jax.ShapeDtypeStruct(full, f32), jax.ShapeDtypeStruct(full, f32)),
+        in_specs=[out, out],
+        out_specs=(hbm, hbm),
+        scratch_shapes=[dma((2, 4))],
+        cost_estimate=pl.CostEstimate(flops=0, bytes_accessed=2_000_000, transcendentals=0),
+    )(volts, stress)
     return volts, stress, rms.reshape(())
 
 

time: 28.1 us -> 61.1 us (2.17)
  Pallas kernels: 24 us -> 57.1 us
    pallas_call x0 -> x1, Pallas kernels: none -> 32.9 us  [body(): pl.pallas_call(deliver, out_shape=(jax.ShapeDtypeStruct(full, f32), jax.S...]
    unnamed x2 -> x4, local copies, waits for them, and re-layouts: 1.59 us -> 1.56 us
where the time goes in v3:
time: 61.1 us; the launch traced here: 61 us
  Pallas kernels  57.1 us (93%)
  between operations  2.35 us (4%)
  local copies, waits for them, and re-layouts  1.56 us (3%)
    pallas_call x1, Pallas kernels, body(): pl.pallas_call(deliver, out_shape=(jax.ShapeDtypeStruct(full, f32), jax.S...  32.9 us
    pallas_call x1, Pallas kernels, body(): pl.pallas_call(functools.partial(kernel, n_x, n_y, layers, rows_x, rows_y...  24.1 us
    unnamed x4, local copies, waits for them, and re-layouts  1.56 us

profile of v3, /device:TPU:0, one launch (start us, length us, event | category | flops | bytes accessed | tf_op | source)
XLA Modules:
  0.0 61.0 jit_solution(16710485201844393954)
XLA Ops:
  0.6 24.1 %shard_map.121 = (f32[8,16,1024]{2,1,0:T(8,128)S(1)}, f32[8,16,1024]{2,1,0:T(8,128)S(1)}, f32[1,1]{1,0:T(1,128)}) custom-call(s32[8]{0:T(128)} %dirs_hbm.1, f32[8,16,1024]{2,1,0:T(8,128)} %volts_hbm.1, f32[8,16,1024]{2,1,0:T(8,128)} %seg_hbm.1, f32[7,16,1024]{2,1,0:T(8,128)} %via_hbm.1, s32[7,16,1024]{2,1,0:T(8,128)} %vmask_hbm.1, s32[16,1024]{1,0:T(8,128)} %pad_hbm.1, ...), custom_call_target="tpu_custom_call" | custom-call | flops 20000000 | bytes 5000000 | tf_op jit(solution)/shard_map/pallas_call | solution.py:415
  24.8 0.0 copy-start
  24.8 0.8 %copy-done = f32[8,16,1024]{2,1,0:T(8,128)} copy-done((f32[8,16,1024]{2,1,0:T(8,128)}, f32[8,16,1024]{2,1,0:T(8,128)S(1)}, u32[]{:S(2)}) %copy-start) | copy-done | bytes 524312
  25.5 0.0 copy-start.1
  25.6 0.8 %copy-done.1 = f32[8,16,1024]{2,1,0:T(8,128)} copy-done((f32[8,16,1024]{2,1,0:T(8,128)}, f32[8,16,1024]{2,1,0:T(8,128)S(1)}, u32[]{:S(2)}) %copy-start.1) | copy-done | bytes 524312
  26.3 32.9 %shard_map.122 = (f32[8,16,1024]{2,1,0:T(8,128)}, f32[8,16,1024]{2,1,0:T(8,128)}) custom-call(f32[8,16,1024]{2,1,0:T(8,128)} %copy-done, f32[8,16,1024]{2,1,0:T(8,128)} %copy-done.1), custom_call_target="tpu_custom_call" | custom-call | bytes 2000000 | tf_op jit(solution)/shard_map/pallas_call | solution.py:442
Async XLA Ops:
  24.8 0.8 %copy-start = (f32[8,16,1024]{2,1,0:T(8,128)}, f32[8,16,1024]{2,1,0:T(8,128)S(1)}, u32[]{:S(2)}) copy-start(f32[8,16,1024]{2,1,0:T(8,128)S(1)} %get-tuple-element.8.volts_ref) | copy-start | bytes 1572868
  25.5 0.8 %copy-start.1 = (f32[8,16,1024]{2,1,0:T(8,128)}, f32[8,16,1024]{2,1,0:T(8,128)S(1)}, u32[]{:S(2)}) copy-start(f32[8,16,1024]{2,1,0:T(8,128)S(1)} %get-tuple-element.9.stress_ref) | copy-start | bytes 1572868

commit v4 on v2

v4 whole, which is shorter than its diff:
```python
import functools
import jax
import jax.numpy as jnp
from jax import lax
from jax.experimental import pallas as pl
from jax.experimental.pallas import tpu as pltpu
from jax.sharding import PartitionSpec as P

damping = 0.8
pad_conductance = 4.0
supply_volts = 1.0
wind_factor = 4.0

MESH = pl.DeviceIdType.MESH
VOLTS, STRESS, PARTIAL, VOLTS2, STRESS1 = range(5)
ROUNDS = 5


def kernel(
    n_x, n_y, n_a, n_b, layers, rows_x, rows_y,
    dirs_hbm, volts_hbm, seg_hbm, via_hbm, vmask_hbm, pad_hbm, load_hbm, stress_hbm, mob_hbm, blk_hbm,
    volts_out, stress_out, rms_out,
    dirs, volts_in, seg_in, via_in, vmask_in, pad_in, load_in, stress_in, mob_in, blk_in,
    cond, via_b, via_a, source, anchor, diag, weight, partial, mob, volts_a, volts_b, stress_a, stress_b,
    volts_fin, stress_fin,
    send_x, recv_x, send_y, recv_y, sum_a, sum_b,
    in_sem, out_sem, send_sem, recv_sem, sa_send, sa_recv, sb_send, sb_recv,
):
    half = layers // 2
    gx = lax.axis_index("gx")
    gy = lax.axis_index("gy")

    moves = [
        pltpu.make_async_copy(src, dst, in_sem.at[i])
        for i, (src, dst) in enumerate(
            [
                (volts_hbm, volts_in), (seg_hbm, seg_in), (via_hbm, via_in), (vmask_hbm, vmask_in), (pad_hbm, pad_in),
                (load_hbm, load_in), (stress_hbm, stress_in), (mob_hbm, mob_in), (blk_hbm, blk_in), (dirs_hbm, dirs),
            ]
        )
    ]
    moves[9].start()
    for move in moves[:9]:
        move.start()

    barrier = pltpu.get_barrier_semaphore()
    me_a, me_b = (gx, gy) if n_b > 1 else (gx * n_y + gy, 0)

    def member(leg, o):
        if leg == 1:
            return gx, lax.rem(gy + o, n_b)
        other = lax.rem(me_a + o, n_a)
        return (other, gy) if n_b > 1 else (other // n_y, lax.rem(other, n_y))

    for leg, n in ((0, n_a), (1, n_b)):
        for o in range(1, n):
            pl.semaphore_signal(barrier, inc=1, device_id=member(leg, o), device_id_type=MESH)

    to_has = [gx < n_x - 1, gx > 0, gy < n_y - 1, gy > 0]
    from_has = [gx > 0, gx < n_x - 1, gy > 0, gy < n_y - 1]
    target = [
        (jnp.minimum(gx + 1, n_x - 1), gy), (jnp.maximum(gx - 1, 0), gy),
        (gx, jnp.minimum(gy + 1, n_y - 1)), (gx, jnp.maximum(gy - 1, 0)),
    ]

    def edge_copy(r, d):
        if d < 2:
            count = 1 if (d == 1 and r in (VOLTS, STRESS)) else 2
            src, dst = send_x.at[r, d, 0:count], recv_x.at[r, d, 0:count]
        else:
            src, dst = send_y.at[r, d - 2], recv_y.at[r, d - 2]
        return pltpu.make_async_remote_copy(
            src_ref=src, dst_ref=dst, send_sem=send_sem.at[r, d], recv_sem=recv_sem.at[r, d],
            device_id=target[d], device_id_type=MESH,
        )

    def start(r, axis):
        if r == VOLTS and axis == 0:
            pl.semaphore_wait(barrier, n_a - 1 + n_b - 1)
        for d in (2 * axis, 2 * axis + 1):
            @pl.when(to_has[d])
            def _():
                edge_copy(r, d).start()

    def arrive(r):
        for d in range(4):
            @pl.when(from_has[d])
            def _():
                edge_copy(r, d).wait_recv()

    for d in range(2):
        @pl.when(jnp.logical_not(from_has[d]))
        def _():
            for r in range(ROUNDS):
                recv_x[r, d] = jnp.full(recv_x.shape[2:], 1.0 if r == PARTIAL else 0.0, jnp.float32)

        @pl.when(jnp.logical_not(from_has[d + 2]))
        def _():
            for r in range(ROUNDS):
                recv_y[r, d] = jnp.full(recv_y.shape[2:], 1.0 if r == PARTIAL else 0.0, jnp.float32)

    moves[9].wait()
    is_y = [dirs[l] for l in range(layers)]
    pos = []
    seen_x, seen_y = jnp.int32(0), jnp.int32(half)
    for l in range(layers):
        pos.append(jnp.where(is_y[l] == 1, seen_y, seen_x))
        seen_y = seen_y + is_y[l]
        seen_x = seen_x + 1 - is_y[l]
    layer = []
    for k in range(layers):
        at = jnp.int32(0)
        for l in range(1, layers):
            at = at + jnp.where(pos[l] == k, l, 0)
        layer.append(at)

    def slot_of(want):
        at = jnp.int32(0)
        for k in range(1, layers):
            at = at + jnp.where(layer[k] == want, k, 0)
        return at

    below = [jnp.maximum(layer[k] - 1, 0) for k in range(layers)]
    above = [jnp.minimum(layer[k] + 1, layers - 1) for k in range(layers)]
    slot_below = [slot_of(below[k]) for k in range(layers)]
    slot_above = [slot_of(above[k]) for k in range(layers)]

    wide = rows_y // 2 if rows_y % 256 == 0 else rows_y
    tall = 8 if rows_x % 8 == 0 else rows_x
    cuts = [
        [(slice(0, rows_x), slice(j, j + wide)) for j in range(0, rows_y, wide)],
        [(slice(i, i + tall), slice(0, rows_y)) for i in range(0, rows_x, tall)],
    ]
    shapes = [(rows_x, wide), (tall, rows_y)]
    length = [rows_x, rows_y]
    index = [lax.broadcasted_iota(jnp.int32, shapes[axis], axis) for axis in range(2)]
    is_first = [index[axis] == 0 for axis in range(2)]
    is_last = [index[axis] == length[axis] - 1 for axis in range(2)]
    outer = [
        jnp.logical_and(is_last[0], gx == n_x - 1),
        jnp.logical_and(is_last[1], gy == n_y - 1),
    ]
    lane = lax.broadcasted_iota(jnp.int32, (tall, 128), 1)

    def pieces(r=None):
        for k in range(layers):
            axis = 0 if k < half else 1
            for rows, cols in cuts[axis]:
                yield k, axis, (rows, cols)
            if r is not None and k == half - 1:
                start(r, 0)
        if r is not None:
            start(r, 1)

    def take(ref, k, p):
        return ref[k, p[0], p[1]]

    def keep(ref, k, p, value):
        ref[k, p[0], p[1]] = value

    def before(a, h, axis):
        return jnp.where(is_first[axis], h, pltpu.roll(a, 1, axis))

    def after(a, h, axis):
        return jnp.where(is_last[axis], h, pltpu.roll(a, length[axis] - 1, axis))

    def first(a, axis):
        return a[0:1, :] if axis == 0 else a[:, 0:1]

    def last(a, axis):
        return a[rows_x - 1:rows_x, :] if axis == 0 else a[:, rows_y - 1:rows_y]

    def put(r, k, p, to_next, to_prev):
        for d, values in ((0, to_next), (1, to_prev)):
            if k < half:
                for i, value in enumerate(values):
                    send_x[r, d, i, k:k + 1, p[1]] = value
            else:
                packed = jnp.broadcast_to(values[0], (tall, 128))
                if len(values) > 1:
                    packed = jnp.where(lane == 0, packed, values[1])
                send_y[r, d, k - half, p[0], :] = packed

    def halo(r, k, p, d, i):
        if k < half:
            return recv_x[r, d, i, k:k + 1, p[1]]
        return recv_y[r, d, k - half, p[0], i:i + 1]

    def fold(a):
        r = a[0:8]
        for i in range(8, a.shape[0], 8):
            r = r + a[i:i + 8]
        out = r[:, 0:128]
        for j in range(128, a.shape[1], 128):
            out = out + r[:, j:j + 128]
        return out

    def sum_copy(leg, o, sender):
        group, me, n, sems = ((sum_a, me_a, n_a, (sa_send, sa_recv)), (sum_b, me_b, n_b, (sb_send, sb_recv)))[leg]
        slot = me if sender else lax.rem(me + o, n)
        return pltpu.make_async_remote_copy(
            src_ref=group.at[me], dst_ref=group.at[slot], send_sem=sems[0].at[o - 1], recv_sem=sems[1].at[slot],
            device_id=member(leg, o), device_id_type=MESH,
        )

    def first_leg():
        for o in range(1, n_a):
            sum_copy(0, o, False).wait_recv()
        along = sum_a[0]
        for i in range(1, n_a):
            along = along + sum_a[i]
        sum_b[me_b] = along
        for o in range(1, n_b):
            sum_copy(1, o, True).start()

    moves[0].wait()
    moves[1].wait()
    for k, axis, p in pieces(VOLTS):
        cr = jnp.where(outer[axis], 0.0, take(seg_in, layer[k], p))
        keep(cond, k, p, cr)
        v = take(volts_in, layer[k], p)
        put(VOLTS, k, p, [last(v, axis), last(cr, axis)], [first(v, axis)])

    def inside(axis, coef, field, minus=None):
        flux = coef * (pltpu.roll(field, length[axis] - 1, axis) - field)
        if minus is not None:
            flux = flux - minus
        flux = jnp.where(is_last[axis], 0.0, flux)
        return flux - pltpu.roll(flux, 1, axis)

    def upright(k, p, v, v_below, v_above):
        return take(via_b, k, p) * v_below + take(via_a, k, p) * v_above + take(source, k, p) - take(anchor, k, p) * v

    for move in moves[2:6]:
        move.wait()
    for k, axis, p in pieces(PARTIAL):
        l = layer[k]
        up = jnp.minimum(l, layers - 2)
        va = take(via_in, up, p) * (take(vmask_in, up, p).astype(jnp.float32) * jnp.where(l < layers - 1, 1.0, 0.0))
        vb = take(via_in, below[k], p) * (take(vmask_in, below[k], p).astype(jnp.float32) * jnp.where(l > 0, 1.0, 0.0))
        pads = pad_conductance * pad_in[p[0], p[1]].astype(jnp.float32)
        top = pads * jnp.where(l == layers - 1, 1.0, 0.0)
        src = top * supply_volts - load_in[p[0], p[1]] * jnp.where(l == 0, 1.0, 0.0)
        hold = va + vb + top
        keep(via_a, k, p, va)
        keep(via_b, k, p, vb)
        keep(source, k, p, src)
        keep(anchor, k, p, hold)
        v = take(volts_in, l, p)
        cr = take(cond, k, p)
        dg = hold + cr + before(cr, 0.0, axis)
        res = inside(axis, cr, v) + vb * take(volts_in, below[k], p) + va * take(volts_in, above[k], p) + src - hold * v
        keep(diag, k, p, dg)
        keep(partial, k, p, res)
        put(PARTIAL, k, p, [last(res, axis), last(dg, axis)], [first(res, axis), first(dg, axis)])

    for move in moves[6:9]:
        move.wait()
    for k, axis, p in pieces(STRESS):
        l = layer[k]
        mr = jnp.where(outer[axis], 0.0, take(mob_in, l, p) * (1.0 - take(blk_in, l, p).astype(jnp.float32)))
        keep(mob, k, p, mr)
        s = take(stress_in, l, p)
        put(STRESS, k, p, [last(s, axis), last(mr, axis)], [first(s, axis)])

    def edge_next(k, p, v_prev, r_prev, v_next, r_next, v):
        axis = 0 if k < half else 1
        c_in, c_out = halo(VOLTS, k, p, 0, 1), last(take(cond, k, p), axis)
        h_prev = v_prev + damping * (r_prev + c_in * (first(v, axis) - v_prev)) / halo(PARTIAL, k, p, 0, 1)
        h_next = v_next + damping * (r_next + c_out * (last(v, axis) - v_next)) / (halo(PARTIAL, k, p, 1, 1) + c_out)
        return h_prev, h_next

    def edges(axis, at_first, at_last):
        return jnp.where(is_first[axis], at_first, jnp.where(is_last[axis], at_last, 0.0))

    arrive(VOLTS)
    for k, axis, p in pieces():
        c_in, c_out = halo(VOLTS, k, p, 0, 1), last(take(cond, k, p), axis)
        v = take(volts_in, layer[k], p)
        w = damping / (take(diag, k, p) + jnp.where(is_first[axis], c_in, 0.0))
        keep(weight, k, p, w)
        cross = edges(
            axis, c_in * (halo(VOLTS, k, p, 0, 0) - first(v, axis)), c_out * (halo(VOLTS, k, p, 1, 0) - last(v, axis))
        )
        keep(volts_a, k, p, v + w * (take(partial, k, p) + cross))

    arrive(PARTIAL)
    for k, axis, p in pieces():
        v = take(volts_a, k, p)
        h_prev, h_next = edge_next(
            k, p, halo(VOLTS, k, p, 0, 0), halo(PARTIAL, k, p, 0, 0), halo(VOLTS, k, p, 1, 0), halo(PARTIAL, k, p, 1, 0),
            take(volts_in, layer[k], p),
        )
        flux = take(cond, k, p) * (after(v, h_next, axis) - v)
        net = flux - before(flux, halo(VOLTS, k, p, 0, 1) * (first(v, axis) - h_prev), axis)
        keep(volts_b, k, p, v + take(weight, k, p) * (net + upright(k, p, v, take(volts_a, slot_below[k], p), take(volts_a, slot_above[k], p))))
    for k, axis, p in pieces(VOLTS2):
        v = take(volts_b, k, p)
        res = inside(axis, take(cond, k, p), v) + upright(k, p, v, take(volts_b, slot_below[k], p), take(volts_b, slot_above[k], p))
        keep(volts_a, k, p, v + take(weight, k, p) * res)
        put(VOLTS2, k, p, [last(v, axis), last(res, axis)], [first(v, axis), first(res, axis)])

    arrive(STRESS)
    for k, axis, p in pieces():
        s = take(stress_in, layer[k], p)
        flux = take(mob, k, p) * (after(s, halo(STRESS, k, p, 1, 0), axis) - s)
        at_first = halo(STRESS, k, p, 0, 1) * (first(s, axis) - halo(STRESS, k, p, 0, 0))
        keep(stress_a, k, p, s + flux - before(flux, at_first, axis))

    arrive(VOLTS2)
    entry, pull = [], []
    for k, axis, p in pieces(STRESS1):
        c_in, c_out = halo(VOLTS, k, p, 0, 1), last(take(cond, k, p), axis)
        v_prev, v_next, v = halo(VOLTS2, k, p, 0, 0), halo(VOLTS2, k, p, 1, 0), take(volts_b, k, p)
        h_prev, h_next = edge_next(k, p, v_prev, halo(VOLTS2, k, p, 0, 1), v_next, halo(VOLTS2, k, p, 1, 1), v)
        cross = edges(axis, c_in * (v_prev - first(v, axis)), c_out * (v_next - last(v, axis)))
        v = take(volts_a, k, p) + take(weight, k, p) * cross
        keep(volts_a, k, p, v)
        flux = take(cond, k, p) * (after(v, h_next, axis) - v)
        keep(partial, k, p, flux)
        at_first = c_in * (first(v, axis) - h_prev)
        mr = take(mob, k, p)
        wind = wind_factor * mr * flux
        keep(diag, k, p, wind)
        wind_first = wind_factor * halo(STRESS, k, p, 0, 1) * at_first
        entry.append(at_first)
        pull.append(wind_first)
        s = take(stress_a, k, p) - wind + before(wind, wind_first, axis)
        keep(stress_a, k, p, s)
        part = s + inside(axis, mr, s, wind)
        keep(stress_b, k, p, part)
        put(STRESS1, k, p, [last(s, axis), last(part, axis)], [first(s, axis), first(part, axis)])

    total = jnp.zeros((8, 128), jnp.float32)
    for i, (k, axis, p) in enumerate(pieces()):
        flux = take(partial, k, p)
        net = flux - before(flux, entry[i], axis)
        res = net + upright(k, p, take(volts_a, k, p), take(volts_a, slot_below[k], p), take(volts_a, slot_above[k], p))
        total = total + fold(res * res)

    sum_a[me_a] = jnp.sum(total, axis=0, keepdims=True)
    for o in range(1, n_a):
        sum_copy(0, o, True).start()

    for l in range(layers):
        volts_fin[l] = volts_a[pos[l]]
    out_v = pltpu.make_async_copy(volts_fin, volts_out, out_sem.at[0])
    out_v.start()

    arrive(STRESS1)
    for i, (k, axis, p) in enumerate(pieces()):
        mr, wind, s = take(mob, k, p), take(diag, k, p), take(stress_a, k, p)
        m_in, m_out = halo(STRESS, k, p, 0, 1), last(mr, axis)
        s_prev, s_next = halo(STRESS1, k, p, 0, 0), halo(STRESS1, k, p, 1, 0)
        flux_in = m_in * (first(s, axis) - s_prev) - pull[i]
        flux_out = m_out * (s_next - last(s, axis)) - last(wind, axis)
        s = take(stress_b, k, p) + edges(axis, -flux_in, flux_out)
        h_prev = halo(STRESS1, k, p, 0, 1) + flux_in
        h_next = halo(STRESS1, k, p, 1, 1) - flux_out
        flux = mr * (after(s, h_next, axis) - s) - wind
        keep(stress_a, k, p, s + flux - before(flux, m_in * (first(s, axis) - h_prev) - pull[i], axis))
        if n_b > 1 and k == half - 1 and p == cuts[0][-1]:
            first_leg()
    for l in range(layers):
        stress_fin[l] = stress_a[pos[l]]
    out_s = pltpu.make_async_copy(stress_fin, stress_out, out_sem.at[1])
    out_s.start()

    if n_b == 1:
        first_leg()
    for o in range(1, n_b):
        sum_copy(1, o, False).wait_recv()
    whole = sum_b[0]
    for i in range(1, n_b):
        whole = whole + sum_b[i]
    nodes = layers * n_x * rows_x * n_y * rows_y
    mean = jnp.sum(whole, keepdims=True) * (1.0 / nodes)
    rms_out[0, 0] = jnp.sqrt(mean)[0, 0]

    for r in range(ROUNDS):
        for d in range(4):
            @pl.when(to_has[d])
            def _():
                edge_copy(r, d).wait_send()
    for leg, n in ((0, n_a), (1, n_b)):
        for o in range(1, n):
            sum_copy(leg, o, True).wait_send()
    out_v.wait()
    out_s.wait()


def body(n_x, n_y, volts_start, seg_cond, via_cond, via_mask, pad_mask, load_current, stress_start, mobility, blocked, layer_dirs):
    layers, rows_x, rows_y = seg_cond.shape
    half = layers // 2
    n_a, n_b = (n_x * n_y, 1) if n_x * n_y <= 64 else (n_x, n_y)
    f32, i32 = jnp.float32, jnp.int32
    full = (layers, rows_x, rows_y)
    vias = via_cond.shape
    flat = (rows_x, rows_y)
    dma = pltpu.SemaphoreType.DMA
    out = pl.BlockSpec(memory_space=pl.ANY)
    hbm = pl.BlockSpec(memory_space=pltpu.HBM)
    operands = (
        layer_dirs, volts_start, seg_cond, via_cond, via_mask, pad_mask, load_current, stress_start, mobility, blocked
    )
    volts, stress, rms = pl.pallas_call(
        functools.partial(kernel, n_x, n_y, n_a, n_b, layers, rows_x, rows_y),
        out_shape=(
            jax.ShapeDtypeStruct(full, f32),
            jax.ShapeDtypeStruct(full, f32),
            jax.ShapeDtypeStruct((1, 1), f32),
        ),
        in_specs=[hbm] * 10,
        out_specs=(out, out, pl.BlockSpec(memory_space=pltpu.SMEM)),
        scratch_shapes=[
            pltpu.SMEM((layers,), i32),
            pltpu.VMEM(full, f32), pltpu.VMEM(full, f32), pltpu.VMEM(vias, f32), pltpu.VMEM(vias, i32),
            pltpu.VMEM(flat, i32), pltpu.VMEM(flat, f32), pltpu.VMEM(full, f32), pltpu.VMEM(full, f32), pltpu.VMEM(full, i32),
        ]
        + [pltpu.VMEM(full, f32)] * 15
        + [
            pltpu.VMEM((ROUNDS, 2, 2, half, rows_y), f32), pltpu.VMEM((ROUNDS, 2, 2, half, rows_y), f32),
            pltpu.VMEM((ROUNDS, 2, half, rows_x, 128), f32), pltpu.VMEM((ROUNDS, 2, half, rows_x, 128), f32),
            pltpu.VMEM((n_a, 1, 128), f32), pltpu.VMEM((n_b, 1, 128), f32),
            dma((10,)), dma((2,)), dma((ROUNDS, 4)), dma((ROUNDS, 4)),
            dma((n_a,)), dma((n_a,)), dma((n_b,)), dma((n_b,)),
        ],
        compiler_params=pltpu.CompilerParams(
            collective_id=0, has_side_effects=True, vmem_limit_bytes=40 * 1024 * 1024
        ),
        cost_estimate=pl.CostEstimate(flops=20_000_000, bytes_accessed=5_000_000, transcendentals=0),
    )(*[pltpu.with_memory_space_constraint(operand, pltpu.HBM) for operand in operands])
    return volts, stress, rms.reshape(())


def solution(mesh):
    tile = P(None, "gx", "gy")
    flat = P("gx", "gy")
    in_specs = (tile, tile, tile, tile, flat, flat, tile, tile, tile, P())
    return jax.shard_map(
        functools.partial(body, mesh.shape["gx"], mesh.shape["gy"]),
        mesh=mesh, in_specs=in_specs, out_specs=(tile, tile, P()), check_vma=False,
    )
```

time: 28.1 us -> 27 us (0.961)
  Pallas kernels: 24 us -> 22.9 us
    pallas_call x1, Pallas kernels: 24 us -> 22.9 us  [body(): pl.pallas_call(functools.partial(kernel, n_x, n_y, n_a, n_b, layers, rows...]
where the time goes in v4:
time: 27 us; the launch traced here: 26.8 us
  Pallas kernels  22.9 us (85%)
  between operations  2.33 us (9%)
  local copies, waits for them, and re-layouts  1.59 us (6%)
    pallas_call x1, Pallas kernels, body(): pl.pallas_call(functools.partial(kernel, n_x, n_y, n_a, n_b, layers, rows...  22.9 us
    unnamed x2, local copies, waits for them, and re-layouts  1.59 us

profile of v4, /device:TPU:0, one launch (start us, length us, event | category | flops | bytes accessed | tf_op | source)
XLA Modules:
  0.0 26.8 jit_solution(15010006352528769205)
XLA Ops:
  0.6 22.9 %shard_map.121 = (f32[8,16,1024]{2,1,0:T(8,128)S(1)}, f32[8,16,1024]{2,1,0:T(8,128)S(1)}, f32[1,1]{1,0:T(1,128)}) custom-call(s32[8]{0:T(128)} %dirs_hbm.1, f32[8,16,1024]{2,1,0:T(8,128)} %volts_hbm.1, f32[8,16,1024]{2,1,0:T(8,128)} %seg_hbm.1, f32[7,16,1024]{2,1,0:T(8,128)} %via_hbm.1, s32[7,16,1024]{2,1,0:T(8,128)} %vmask_hbm.1, s32[16,1024]{1,0:T(8,128)} %pad_hbm.1, ...), custom_call_target="tpu_custom_call" | custom-call | flops 20000000 | bytes 5000000 | tf_op jit(solution)/shard_map/pallas_call | solution.py:406
  23.5 0.8 %copy.16 = f32[8,16,1024]{2,1,0:T(8,128)} copy(f32[8,16,1024]{2,1,0:T(8,128)S(1)} %get-tuple-element.12) | data formatting | bytes 1048576
  24.3 0.8 %copy.17 = f32[8,16,1024]{2,1,0:T(8,128)} copy(f32[8,16,1024]{2,1,0:T(8,128)S(1)} %get-tuple-element.13) | data formatting | bytes 1048576

commit v5 on v4

--- a/solution.py
+++ b/solution.py
@@ -40,7 +40,7 @@
         )
     ]
     moves[9].start()
-    for move in moves[:9]:
+    for move in moves[:6]:
         move.start()
 
     barrier = pltpu.get_barrier_semaphore()
@@ -82,8 +82,8 @@
             def _():
                 edge_copy(r, d).start()
 
-    def arrive(r):
-        for d in range(4):
+    def arrive(r, axis):
+        for d in (2 * axis, 2 * axis + 1):
             @pl.when(from_has[d])
             def _():
                 edge_copy(r, d).wait_recv()
@@ -142,15 +142,18 @@
     ]
     lane = lax.broadcasted_iota(jnp.int32, (tall, 128), 1)
 
-    def pieces(r=None):
-        for k in range(layers):
-            axis = 0 if k < half else 1
-            for rows, cols in cuts[axis]:
-                yield k, axis, (rows, cols)
-            if r is not None and k == half - 1:
-                start(r, 0)
-        if r is not None:
-            start(r, 1)
+    def pieces(send=None, recv=None):
+        for axis in (0, 1) if recv is None else (1, 0):
+            if recv is not None:
+                arrive(recv, axis)
+            for k in range(axis * half, axis * half + half):
+                for rows, cols in cuts[axis]:
+                    yield k, axis, (rows, cols)
+            if send is not None:
+                start(send, axis)
+
+    def key(k, p):
+        return k, p[0].start, p[1].start
 
     def take(ref, k, p):
         return ref[k, p[0], p[1]]
@@ -233,6 +236,8 @@
 
     for move in moves[2:6]:
         move.wait()
+    for move in moves[6:9]:
+        move.start()
     for k, axis, p in pieces(PARTIAL):
         l = layer[k]
         up = jnp.minimum(l, layers - 2)
@@ -273,8 +278,7 @@
     def edges(axis, at_first, at_last):
         return jnp.where(is_first[axis], at_first, jnp.where(is_last[axis], at_last, 0.0))
 
-    arrive(VOLTS)
-    for k, axis, p in pieces():
+    for k, axis, p in pieces(recv=VOLTS):
         c_in, c_out = halo(VOLTS, k, p, 0, 1), last(take(cond, k, p), axis)
         v = take(volts_in, layer[k], p)
         w = damping / (take(diag, k, p) + jnp.where(is_first[axis], c_in, 0.0))
@@ -284,8 +288,7 @@
         )
         keep(volts_a, k, p, v + w * (take(partial, k, p) + cross))
 
-    arrive(PARTIAL)
-    for k, axis, p in pieces():
+    for k, axis, p in pieces(recv=PARTIAL):
         v = take(volts_a, k, p)
         h_prev, h_next = edge_next(
             k, p, halo(VOLTS, k, p, 0, 0), halo(PARTIAL, k, p, 0, 0), halo(VOLTS, k, p, 1, 0), halo(PARTIAL, k, p, 1, 0),
@@ -300,16 +303,14 @@
         keep(volts_a, k, p, v + take(weight, k, p) * res)
         put(VOLTS2, k, p, [last(v, axis), last(res, axis)], [first(v, axis), first(res, axis)])
 
-    arrive(STRESS)
-    for k, axis, p in pieces():
+    for k, axis, p in pieces(recv=STRESS):
         s = take(stress_in, layer[k], p)
         flux = take(mob, k, p) * (after(s, halo(STRESS, k, p, 1, 0), axis) - s)
         at_first = halo(STRESS, k, p, 0, 1) * (first(s, axis) - halo(STRESS, k, p, 0, 0))
         keep(stress_a, k, p, s + flux - before(flux, at_first, axis))
 
-    arrive(VOLTS2)
-    entry, pull = [], []
-    for k, axis, p in pieces(STRESS1):
+    entry, pull = {}, {}
+    for k, axis, p in pieces(send=STRESS1, recv=VOLTS2):
         c_in, c_out = halo(VOLTS, k, p, 0, 1), last(take(cond, k, p), axis)
         v_prev, v_next, v = halo(VOLTS2, k, p, 0, 0), halo(VOLTS2, k, p, 1, 0), take(volts_b, k, p)
         h_prev, h_next = edge_next(k, p, v_prev, halo(VOLTS2, k, p, 0, 1), v_next, halo(VOLTS2, k, p, 1, 1), v)
@@ -323,8 +324,8 @@
         wind = wind_factor * mr * flux
         keep(diag, k, p, wind)
         wind_first = wind_factor * halo(STRESS, k, p, 0, 1) * at_first
-        entry.append(at_first)
-        pull.append(wind_first)
+        entry[key(k, p)] = at_first
+        pull[key(k, p)] = wind_first
         s = take(stress_a, k, p) - wind + before(wind, wind_first, axis)
         keep(stress_a, k, p, s)
         part = s + inside(axis, mr, s, wind)
@@ -332,9 +333,9 @@
         put(STRESS1, k, p, [last(s, axis), last(part, axis)], [first(s, axis), first(part, axis)])
 
     total = jnp.zeros((8, 128), jnp.float32)
-    for i, (k, axis, p) in enumerate(pieces()):
+    for k, axis, p in pieces():
         flux = take(partial, k, p)
-        net = flux - before(flux, entry[i], axis)
+        net = flux - before(flux, entry[key(k, p)], axis)
         res = net + upright(k, p, take(volts_a, k, p), take(volts_a, slot_below[k], p), take(volts_a, slot_above[k], p))
         total = total + fold(res * res)
 
@@ -347,19 +348,18 @@
     out_v = pltpu.make_async_copy(volts_fin, volts_out, out_sem.at[0])
     out_v.start()
 
-    arrive(STRESS1)
-    for i, (k, axis, p) in enumerate(pieces()):
+    for k, axis, p in pieces(recv=STRESS1):
         mr, wind, s = take(mob, k, p), take(diag, k, p), take(stress_a, k, p)
         m_in, m_out = halo(STRESS, k, p, 0, 1), last(mr, axis)
         s_prev, s_next = halo(STRESS1, k, p, 0, 0), halo(STRESS1, k, p, 1, 0)
-        flux_in = m_in * (first(s, axis) - s_prev) - pull[i]
+        flux_in = m_in * (first(s, axis) - s_prev) - pull[key(k, p)]
         flux_out = m_out * (s_next - last(s, axis)) - last(wind, axis)
         s = take(stress_b, k, p) + edges(axis, -flux_in, flux_out)
         h_prev = halo(STRESS1, k, p, 0, 1) + flux_in
         h_next = halo(STRESS1, k, p, 1, 1) - flux_out
         flux = mr * (after(s, h_next, axis) - s) - wind
-        keep(stress_a, k, p, s + flux - before(flux, m_in * (first(s, axis) - h_prev) - pull[i], axis))
-        if n_b > 1 and k == half - 1 and p == cuts[0][-1]:
+        keep(stress_a, k, p, s + flux - before(flux, m_in * (first(s, axis) - h_prev) - pull[key(k, p)], axis))
+        if n_b > 1 and k == layers - 1 and p == cuts[1][-1]:
             first_leg()
     for l in range(layers):
         stress_fin[l] = stress_a[pos[l]]
@@ -387,6 +387,20 @@
             sum_copy(leg, o, True).wait_send()
     out_v.wait()
     out_s.wait()
+
+
+def deliver(volts_ref, stress_ref, volts_out, stress_out, sems):
+    parts = sems.shape[1]
+    count = volts_ref.shape[0] // parts
+    moves = [
+        pltpu.make_async_copy(src.at[i * count:(i + 1) * count], dst.at[i * count:(i + 1) * count], sems.at[j, i])
+        for j, (src, dst) in enumerate([(volts_ref, volts_out), (stress_ref, stress_out)])
+        for i in range(parts)
+    ]
+    for move in moves:
+        move.start()
+    for move in moves:
+        move.wait()
 
 
 def body(n_x, n_y, volts_start, seg_cond, via_cond, via_mask, pad_mask, load_current, stress_start, mobility, blocked, layer_dirs):
@@ -430,6 +444,15 @@
         ),
         cost_estimate=pl.CostEstimate(flops=20_000_000, bytes_accessed=5_000_000, transcendentals=0),
     )(*[pltpu.with_memory_space_constraint(operand, pltpu.HBM) for operand in operands])
+    volts, stress = pl.pallas_call(
+        deliver,
+        out_shape=(jax.ShapeDtypeStruct(full, f32), jax.ShapeDtypeStruct(full, f32)),
+        in_specs=[out, out],
+        out_specs=(hbm, hbm),
+        scratch_shapes=[dma((2, 4))],
+        compiler_params=pltpu.CompilerParams(vmem_limit_bytes=2 * 1024 * 1024),
+        cost_estimate=pl.CostEstimate(flops=0, bytes_accessed=2_000_000, transcendentals=0),
+    )(volts, stress)
     return volts, stress, rms.reshape(())
 
 

time: 27 us -> 25.1 us (0.930)
  local copies, waits for them, and re-layouts: 1.59 us -> 0 us
  Pallas kernels: 22.9 us -> 22.5 us
    unnamed x2 -> x0, local copies, waits for them, and re-layouts: 1.59 us -> none
    pallas_call x1, Pallas kernels: 22.9 us -> 21.5 us  [body(): pl.pallas_call(functools.partial(kernel, n_x, n_y, n_a, n_b, layers, rows...]
    pallas_call x0 -> x1, Pallas kernels: none -> 1.03 us  [body(): pl.pallas_call(deliver, out_shape=(jax.ShapeDtypeStruct(full, f32), jax.S...]
where the time goes in v5:
time: 25.1 us; the launch traced here: 24.9 us
  Pallas kernels  22.5 us (90%)
  between operations  2.41 us (10%)
    pallas_call x1, Pallas kernels, body(): pl.pallas_call(functools.partial(kernel, n_x, n_y, n_a, n_b, layers, rows...  21.5 us
    pallas_call x1, Pallas kernels, body(): pl.pallas_call(deliver, out_shape=(jax.ShapeDtypeStruct(full, f32), jax.S...  1.03 us

profile of v5, /device:TPU:0, one launch (start us, length us, event | category | flops | bytes accessed | tf_op | source)
XLA Modules:
  0.0 24.9 jit_solution(8896507357633713026)
XLA Ops:
  0.6 21.5 %shard_map.121 = (f32[8,16,1024]{2,1,0:T(8,128)S(1)}, f32[8,16,1024]{2,1,0:T(8,128)S(1)}, f32[1,1]{1,0:T(1,128)}) custom-call(s32[8]{0:T(128)} %dirs_hbm.1, f32[8,16,1024]{2,1,0:T(8,128)} %volts_hbm.1, f32[8,16,1024]{2,1,0:T(8,128)} %seg_hbm.1, f32[7,16,1024]{2,1,0:T(8,128)} %via_hbm.1, s32[7,16,1024]{2,1,0:T(8,128)} %vmask_hbm.1, s32[16,1024]{1,0:T(8,128)} %pad_hbm.1, ...), custom_call_target="tpu_custom_call" | custom-call | flops 20000000 | bytes 5000000 | tf_op jit(solution)/shard_map/pallas_call | solution.py:420
  22.2 1.0 %shard_map.122 = (f32[8,16,1024]{2,1,0:T(8,128)}, f32[8,16,1024]{2,1,0:T(8,128)}) custom-call(f32[8,16,1024]{2,1,0:T(8,128)S(1)} %get-tuple-element.8.volts_ref, f32[8,16,1024]{2,1,0:T(8,128)S(1)} %get-tuple-element.9.stress_ref), custom_call_target="tpu_custom_call" | custom-call | bytes 2000000 | tf_op jit(solution)/shard_map/pallas_call | solution.py:447

commit v6 on v5

--- a/solution.py
+++ b/solution.py
@@ -63,30 +63,37 @@
         (gx, jnp.minimum(gy + 1, n_y - 1)), (gx, jnp.maximum(gy - 1, 0)),
     ]
 
-    def edge_copy(r, d):
+    def edge_copy(r, d, i):
         if d < 2:
-            count = 1 if (d == 1 and r in (VOLTS, STRESS)) else 2
-            src, dst = send_x.at[r, d, 0:count], recv_x.at[r, d, 0:count]
+            src, dst, sem = send_x.at[r, d, i], recv_x.at[r, d, i], 2 * d + i
         else:
-            src, dst = send_y.at[r, d - 2], recv_y.at[r, d - 2]
+            src, dst, sem = send_y.at[r, d - 2], recv_y.at[r, d - 2], 2 + d
         return pltpu.make_async_remote_copy(
-            src_ref=src, dst_ref=dst, send_sem=send_sem.at[r, d], recv_sem=recv_sem.at[r, d],
+            src_ref=src, dst_ref=dst, send_sem=send_sem.at[r, sem], recv_sem=recv_sem.at[r, sem],
             device_id=target[d], device_id_type=MESH,
         )
 
-    def start(r, axis):
+    def copies(r, d):
+        if d >= 2 or (d == 1 and r in (VOLTS, STRESS)):
+            return (0,)
+        return (0, 1)
+
+    def start(r, axis, which=(0, 1)):
         if r == VOLTS and axis == 0:
             pl.semaphore_wait(barrier, n_a - 1 + n_b - 1)
         for d in (2 * axis, 2 * axis + 1):
             @pl.when(to_has[d])
             def _():
-                edge_copy(r, d).start()
+                for i in copies(r, d):
+                    if axis == 1 or i in which:
+                        edge_copy(r, d, i).start()
 
     def arrive(r, axis):
         for d in (2 * axis, 2 * axis + 1):
             @pl.when(from_has[d])
             def _():
-                edge_copy(r, d).wait_recv()
+                for i in copies(r, d):
+                    edge_copy(r, d, i).wait_recv()
 
     for d in range(2):
         @pl.when(jnp.logical_not(from_has[d]))
@@ -142,15 +149,18 @@
     ]
     lane = lax.broadcasted_iota(jnp.int32, (tall, 128), 1)
 
-    def pieces(send=None, recv=None):
+    def pieces_of(axis):
+        for k in range(axis * half, axis * half + half):
+            for rows, cols in cuts[axis]:
+                yield k, axis, (rows, cols)
+
+    def pieces(send=None, recv=None, which=(0, 1)):
         for axis in (0, 1) if recv is None else (1, 0):
             if recv is not None:
                 arrive(recv, axis)
-            for k in range(axis * half, axis * half + half):
-                for rows, cols in cuts[axis]:
-                    yield k, axis, (rows, cols)
+            yield from pieces_of(axis)
             if send is not None:
-                start(send, axis)
+                start(send, axis, which)
 
     def key(k, p):
         return k, p[0].start, p[1].start
@@ -173,11 +183,11 @@
     def last(a, axis):
         return a[rows_x - 1:rows_x, :] if axis == 0 else a[:, rows_y - 1:rows_y]
 
-    def put(r, k, p, to_next, to_prev):
+    def put(r, k, p, to_next, to_prev, base=0):
         for d, values in ((0, to_next), (1, to_prev)):
             if k < half:
                 for i, value in enumerate(values):
-                    send_x[r, d, i, k:k + 1, p[1]] = value
+                    send_x[r, d, base + i, k:k + 1, p[1]] = value
             else:
                 packed = jnp.broadcast_to(values[0], (tall, 128))
                 if len(values) > 1:
@@ -238,26 +248,38 @@
         move.wait()
     for move in moves[6:9]:
         move.start()
-    for k, axis, p in pieces(PARTIAL):
-        l = layer[k]
-        up = jnp.minimum(l, layers - 2)
-        va = take(via_in, up, p) * (take(vmask_in, up, p).astype(jnp.float32) * jnp.where(l < layers - 1, 1.0, 0.0))
-        vb = take(via_in, below[k], p) * (take(vmask_in, below[k], p).astype(jnp.float32) * jnp.where(l > 0, 1.0, 0.0))
-        pads = pad_conductance * pad_in[p[0], p[1]].astype(jnp.float32)
-        top = pads * jnp.where(l == layers - 1, 1.0, 0.0)
-        src = top * supply_volts - load_in[p[0], p[1]] * jnp.where(l == 0, 1.0, 0.0)
-        hold = va + vb + top
-        keep(via_a, k, p, va)
-        keep(via_b, k, p, vb)
-        keep(source, k, p, src)
-        keep(anchor, k, p, hold)
-        v = take(volts_in, l, p)
-        cr = take(cond, k, p)
-        dg = hold + cr + before(cr, 0.0, axis)
-        res = inside(axis, cr, v) + vb * take(volts_in, below[k], p) + va * take(volts_in, above[k], p) + src - hold * v
-        keep(diag, k, p, dg)
-        keep(partial, k, p, res)
-        put(PARTIAL, k, p, [last(res, axis), last(dg, axis)], [first(res, axis), first(dg, axis)])
+    for along in (0, 1):
+        for k, axis, p in pieces_of(along):
+            l = layer[k]
+            up = jnp.minimum(l, layers - 2)
+            va = take(via_in, up, p) * (take(vmask_in, up, p).astype(jnp.float32) * jnp.where(l < layers - 1, 1.0, 0.0))
+            vb = take(via_in, below[k], p) * (take(vmask_in, below[k], p).astype(jnp.float32) * jnp.where(l > 0, 1.0, 0.0))
+            pads = pad_conductance * pad_in[p[0], p[1]].astype(jnp.float32)
+            top = pads * jnp.where(l == layers - 1, 1.0, 0.0)
+            src = top * supply_volts - load_in[p[0], p[1]] * jnp.where(l == 0, 1.0, 0.0)
+            hold = va + vb + top
+            keep(via_a, k, p, va)
+            keep(via_b, k, p, vb)
+            keep(source, k, p, src)
+            keep(anchor, k, p, hold)
+            cr = take(cond, k, p)
+            dg = hold + cr + before(cr, 0.0, axis)
+            keep(diag, k, p, dg)
+            if axis == 0:
+                put(PARTIAL, k, p, [last(dg, axis)], [first(dg, axis)], 1)
+        if along == 0:
+            start(PARTIAL, 0, (1,))
+        for k, axis, p in pieces_of(along):
+            l = layer[k]
+            v, cr, dg = take(volts_in, l, p), take(cond, k, p), take(diag, k, p)
+            va, vb, src, hold = take(via_a, k, p), take(via_b, k, p), take(source, k, p), take(anchor, k, p)
+            res = inside(axis, cr, v) + vb * take(volts_in, below[k], p) + va * take(volts_in, above[k], p) + src - hold * v
+            keep(partial, k, p, res)
+            if axis == 0:
+                put(PARTIAL, k, p, [last(res, axis)], [first(res, axis)])
+            else:
+                put(PARTIAL, k, p, [last(res, axis), last(dg, axis)], [first(res, axis), first(dg, axis)])
+        start(PARTIAL, along, (0,))
 
     for move in moves[6:9]:
         move.wait()
@@ -296,12 +318,20 @@
         )
         flux = take(cond, k, p) * (after(v, h_next, axis) - v)
         net = flux - before(flux, halo(VOLTS, k, p, 0, 1) * (first(v, axis) - h_prev), axis)
-        keep(volts_b, k, p, v + take(weight, k, p) * (net + upright(k, p, v, take(volts_a, slot_below[k], p), take(volts_a, slot_above[k], p))))
-    for k, axis, p in pieces(VOLTS2):
+        net = net + upright(k, p, v, take(volts_a, slot_below[k], p), take(volts_a, slot_above[k], p))
+        v = v + take(weight, k, p) * net
+        keep(volts_b, k, p, v)
+        if axis == 0:
+            put(VOLTS2, k, p, [last(v, axis)], [first(v, axis)])
+    start(VOLTS2, 0, (0,))
+    for k, axis, p in pieces(VOLTS2, which=(1,)):
         v = take(volts_b, k, p)
         res = inside(axis, take(cond, k, p), v) + upright(k, p, v, take(volts_b, slot_below[k], p), take(volts_b, slot_above[k], p))
         keep(volts_a, k, p, v + take(weight, k, p) * res)
-        put(VOLTS2, k, p, [last(v, axis), last(res, axis)], [first(v, axis), first(res, axis)])
+        if axis == 0:
+            put(VOLTS2, k, p, [last(res, axis)], [first(res, axis)], 1)
+        else:
+            put(VOLTS2, k, p, [last(v, axis), last(res, axis)], [first(v, axis), first(res, axis)])
 
     for k, axis, p in pieces(recv=STRESS):
         s = take(stress_in, layer[k], p)
@@ -310,7 +340,7 @@
         keep(stress_a, k, p, s + flux - before(flux, at_first, axis))
 
     entry, pull = {}, {}
-    for k, axis, p in pieces(send=STRESS1, recv=VOLTS2):
+    for k, axis, p in pieces(send=STRESS1, recv=VOLTS2, which=(0,)):
         c_in, c_out = halo(VOLTS, k, p, 0, 1), last(take(cond, k, p), axis)
         v_prev, v_next, v = halo(VOLTS2, k, p, 0, 0), halo(VOLTS2, k, p, 1, 0), take(volts_b, k, p)
         h_prev, h_next = edge_next(k, p, v_prev, halo(VOLTS2, k, p, 0, 1), v_next, halo(VOLTS2, k, p, 1, 1), v)
@@ -328,9 +358,18 @@
         pull[key(k, p)] = wind_first
         s = take(stress_a, k, p) - wind + before(wind, wind_first, axis)
         keep(stress_a, k, p, s)
+        if axis == 0:
+            put(STRESS1, k, p, [last(s, axis)], [first(s, axis)])
+            continue
         part = s + inside(axis, mr, s, wind)
         keep(stress_b, k, p, part)
         put(STRESS1, k, p, [last(s, axis), last(part, axis)], [first(s, axis), first(part, axis)])
+    for k, axis, p in pieces_of(0):
+        s = take(stress_a, k, p)
+        part = s + inside(axis, take(mob, k, p), s, take(diag, k, p))
+        keep(stress_b, k, p, part)
+        put(STRESS1, k, p, [last(part, axis)], [first(part, axis)], 1)
+    start(STRESS1, 0, (1,))
 
     total = jnp.zeros((8, 128), jnp.float32)
     for k, axis, p in pieces():
@@ -361,10 +400,12 @@
         keep(stress_a, k, p, s + flux - before(flux, m_in * (first(s, axis) - h_prev) - pull[key(k, p)], axis))
         if n_b > 1 and k == layers - 1 and p == cuts[1][-1]:
             first_leg()
-    for l in range(layers):
+    out_s = []
+    for l in range(0, layers, 2):
         stress_fin[l] = stress_a[pos[l]]
-    out_s = pltpu.make_async_copy(stress_fin, stress_out, out_sem.at[1])
-    out_s.start()
+        stress_fin[l + 1] = stress_a[pos[l + 1]]
+        out_s.append(pltpu.make_async_copy(stress_fin.at[l:l + 2], stress_out.at[l:l + 2], out_sem.at[1 + l // 2]))
+        out_s[-1].start()
 
     if n_b == 1:
         first_leg()
@@ -381,12 +422,14 @@
         for d in range(4):
             @pl.when(to_has[d])
             def _():
-                edge_copy(r, d).wait_send()
+                for i in copies(r, d):
+                    edge_copy(r, d, i).wait_send()
     for leg, n in ((0, n_a), (1, n_b)):
         for o in range(1, n):
             sum_copy(leg, o, True).wait_send()
     out_v.wait()
-    out_s.wait()
+    for move in out_s:
+        move.wait()
 
 
 def deliver(volts_ref, stress_ref, volts_out, stress_out, sems):
@@ -436,7 +479,7 @@
             pltpu.VMEM((ROUNDS, 2, 2, half, rows_y), f32), pltpu.VMEM((ROUNDS, 2, 2, half, rows_y), f32),
             pltpu.VMEM((ROUNDS, 2, half, rows_x, 128), f32), pltpu.VMEM((ROUNDS, 2, half, rows_x, 128), f32),
             pltpu.VMEM((n_a, 1, 128), f32), pltpu.VMEM((n_b, 1, 128), f32),
-            dma((10,)), dma((2,)), dma((ROUNDS, 4)), dma((ROUNDS, 4)),
+            dma((10,)), dma((1 + half,)), dma((ROUNDS, 6)), dma((ROUNDS, 6)),
             dma((n_a,)), dma((n_a,)), dma((n_b,)), dma((n_b,)),
         ],
         compiler_params=pltpu.CompilerParams(

time: 25.1 us -> 25.6 us (1.020)
  Pallas kernels: 22.5 us -> 22.8 us
    pallas_call x1, Pallas kernels: 21.5 us -> 21.8 us  [body(): pl.pallas_call(functools.partial(kernel, n_x, n_y, n_a, n_b, layers, rows...]
where the time goes in v6:
time: 25.6 us; the launch traced here: 25.2 us
  Pallas kernels  22.8 us (89%)
  between operations  2.41 us (9%)
    pallas_call x1, Pallas kernels, body(): pl.pallas_call(functools.partial(kernel, n_x, n_y, n_a, n_b, layers, rows...  21.8 us
    pallas_call x1, Pallas kernels, body(): pl.pallas_call(deliver, out_shape=(jax.ShapeDtypeStruct(full, f32), jax.S...  1.03 us

profile of v6, /device:TPU:0, one launch (start us, length us, event | category | flops | bytes accessed | tf_op | source)
XLA Modules:
  0.0 25.2 jit_solution(14311299007526560285)
XLA Ops:
  0.6 21.8 %shard_map.121 = (f32[8,16,1024]{2,1,0:T(8,128)S(1)}, f32[8,16,1024]{2,1,0:T(8,128)S(1)}, f32[1,1]{1,0:T(1,128)}) custom-call(s32[8]{0:T(128)} %dirs_hbm.1, f32[8,16,1024]{2,1,0:T(8,128)} %volts_hbm.1, f32[8,16,1024]{2,1,0:T(8,128)} %seg_hbm.1, f32[7,16,1024]{2,1,0:T(8,128)} %via_hbm.1, s32[7,16,1024]{2,1,0:T(8,128)} %vmask_hbm.1, s32[16,1024]{1,0:T(8,128)} %pad_hbm.1, ...), custom_call_target="tpu_custom_call" | custom-call | flops 20000000 | bytes 5000000 | tf_op jit(solution)/shard_map/pallas_call | solution.py:463
  22.4 1.0 %shard_map.122 = (f32[8,16,1024]{2,1,0:T(8,128)}, f32[8,16,1024]{2,1,0:T(8,128)}) custom-call(f32[8,16,1024]{2,1,0:T(8,128)S(1)} %get-tuple-element.8.volts_ref, f32[8,16,1024]{2,1,0:T(8,128)S(1)} %get-tuple-element.9.stress_ref), custom_call_target="tpu_custom_call" | custom-call | bytes 2000000 | tf_op jit(solution)/shard_map/pallas_call | solution.py:490

commit v7 on v5

--- a/solution.py
+++ b/solution.py
@@ -87,6 +87,12 @@
             @pl.when(from_has[d])
             def _():
                 edge_copy(r, d).wait_recv()
+
+    def sent(r):
+        for d in range(4):
+            @pl.when(to_has[d])
+            def _():
+                edge_copy(r, d).wait_send()
 
     for d in range(2):
         @pl.when(jnp.logical_not(from_has[d]))
@@ -348,6 +354,9 @@
     out_v = pltpu.make_async_copy(volts_fin, volts_out, out_sem.at[0])
     out_v.start()
 
+    for r in (VOLTS, PARTIAL, STRESS, VOLTS2):
+        sent(r)
+
     for k, axis, p in pieces(recv=STRESS1):
         mr, wind, s = take(mob, k, p), take(diag, k, p), take(stress_a, k, p)
         m_in, m_out = halo(STRESS, k, p, 0, 1), last(mr, axis)
@@ -361,10 +370,12 @@
         keep(stress_a, k, p, s + flux - before(flux, m_in * (first(s, axis) - h_prev) - pull[key(k, p)], axis))
         if n_b > 1 and k == layers - 1 and p == cuts[1][-1]:
             first_leg()
-    for l in range(layers):
+    out_s = []
+    for l in range(0, layers, 2):
         stress_fin[l] = stress_a[pos[l]]
-    out_s = pltpu.make_async_copy(stress_fin, stress_out, out_sem.at[1])
-    out_s.start()
+        stress_fin[l + 1] = stress_a[pos[l + 1]]
+        out_s.append(pltpu.make_async_copy(stress_fin.at[l:l + 2], stress_out.at[l:l + 2], out_sem.at[1 + l // 2]))
+        out_s[-1].start()
 
     if n_b == 1:
         first_leg()
@@ -377,16 +388,13 @@
     mean = jnp.sum(whole, keepdims=True) * (1.0 / nodes)
     rms_out[0, 0] = jnp.sqrt(mean)[0, 0]
 
-    for r in range(ROUNDS):
-        for d in range(4):
-            @pl.when(to_has[d])
-            def _():
-                edge_copy(r, d).wait_send()
+    sent(STRESS1)
     for leg, n in ((0, n_a), (1, n_b)):
         for o in range(1, n):
             sum_copy(leg, o, True).wait_send()
     out_v.wait()
-    out_s.wait()
+    for move in out_s:
+        move.wait()
 
 
 def deliver(volts_ref, stress_ref, volts_out, stress_out, sems):
@@ -436,7 +444,7 @@
             pltpu.VMEM((ROUNDS, 2, 2, half, rows_y), f32), pltpu.VMEM((ROUNDS, 2, 2, half, rows_y), f32),
             pltpu.VMEM((ROUNDS, 2, half, rows_x, 128), f32), pltpu.VMEM((ROUNDS, 2, half, rows_x, 128), f32),
             pltpu.VMEM((n_a, 1, 128), f32), pltpu.VMEM((n_b, 1, 128), f32),
-            dma((10,)), dma((2,)), dma((ROUNDS, 4)), dma((ROUNDS, 4)),
+            dma((10,)), dma((1 + half,)), dma((ROUNDS, 4)), dma((ROUNDS, 4)),
             dma((n_a,)), dma((n_a,)), dma((n_b,)), dma((n_b,)),
         ],
         compiler_params=pltpu.CompilerParams(

time: 25.1 us -> 25.8 us (1.028)
  Pallas kernels: 22.5 us -> 23.2 us
    pallas_call x1, Pallas kernels: 21.5 us -> 22.1 us  [body(): pl.pallas_call(functools.partial(kernel, n_x, n_y, n_a, n_b, layers, rows...]
where the time goes in v7:
time: 25.8 us; the launch traced here: 25.6 us
  Pallas kernels  23.2 us (90%)
  between operations  2.41 us (9%)
    pallas_call x1, Pallas kernels, body(): pl.pallas_call(functools.partial(kernel, n_x, n_y, n_a, n_b, layers, rows...  22.1 us
    pallas_call x1, Pallas kernels, body(): pl.pallas_call(deliver, out_shape=(jax.ShapeDtypeStruct(full, f32), jax.S...  1.03 us

profile of v7, /device:TPU:0, one launch (start us, length us, event | category | flops | bytes accessed | tf_op | source)
XLA Modules:
  0.0 25.6 jit_solution(14844001997138426510)
XLA Ops:
  0.6 22.1 %shard_map.121 = (f32[8,16,1024]{2,1,0:T(8,128)S(1)}, f32[8,16,1024]{2,1,0:T(8,128)S(1)}, f32[1,1]{1,0:T(1,128)}) custom-call(s32[8]{0:T(128)} %dirs_hbm.1, f32[8,16,1024]{2,1,0:T(8,128)} %volts_hbm.1, f32[8,16,1024]{2,1,0:T(8,128)} %seg_hbm.1, f32[7,16,1024]{2,1,0:T(8,128)} %via_hbm.1, s32[7,16,1024]{2,1,0:T(8,128)} %vmask_hbm.1, s32[16,1024]{1,0:T(8,128)} %pad_hbm.1, ...), custom_call_target="tpu_custom_call" | custom-call | flops 20000000 | bytes 5000000 | tf_op jit(solution)/shard_map/pallas_call | solution.py:428
  22.8 1.0 %shard_map.122 = (f32[8,16,1024]{2,1,0:T(8,128)}, f32[8,16,1024]{2,1,0:T(8,128)}) custom-call(f32[8,16,1024]{2,1,0:T(8,128)S(1)} %get-tuple-element.8.volts_ref, f32[8,16,1024]{2,1,0:T(8,128)S(1)} %get-tuple-element.9.stress_ref), custom_call_target="tpu_custom_call" | custom-call | bytes 2000000 | tf_op jit(solution)/shard_map/pallas_call | solution.py:455
